TPU v7x, 32 devices: a whole 2x2x4 slice. The times are simulated.
32 devices in a mesh: row: 4 (over y, x), col: 8 (over z, core).
Axes of the slice: x: 2, y: 2, z: 4, core: 2. Of those that a mesh axis runs over, the one named last changes fastest.
Arguments:
- activations: bfloat16 [512, 28672], P('col', 'row'), may hold values from -6 to 6
- act_basis: bfloat16 [28672, 28672], P('row', 'col'), may hold values from -0.03125 to 0.03125
- out_grads: bfloat16 [512, 8192], P('row', 'col'), may hold values from -0.375 to 0.375
- grad_basis: bfloat16 [8192, 8192], P('col', 'row'), may hold values from -0.0625 to 0.0625
Outputs:
- eigen_lambda: bfloat16 [8192, 28672], P('row', 'col')
All inputs are finite; a program needn't handle non-finite values.
Results may differ from a plain program's by a relative error of at most 0.0058.
Values may be sent and summed in bfloat16 or wider, within the bound.
No kernel may reach another device: no remote copies, remote signals or barrier semaphores. Data moves between devices by JAX's collectives and lax.ppermute only.
A program may use at most 192 MiB of HBM per device.

v0:
```python
import functools

import jax
import jax.numpy as jnp
import numpy as np
from jax import lax
from jax.experimental import pallas as pl
from jax.experimental.pallas import tpu as pltpu
from jax.sharding import PartitionSpec as P

SEQS = 2
CORES = 2
F32 = jnp.float32
BF16 = jnp.bfloat16
ANYWHERE = pl.BlockSpec(memory_space=pl.ANY)
IN_VMEM = pl.BlockSpec(memory_space=pltpu.VMEM)


def vmem(mib):
    return pltpu.CompilerParams(vmem_limit_bytes=mib * 2**20)


def largest_tile(size, unit, most):
    tile = unit
    for candidate in range(unit, most + 1, unit):
        if size % candidate == 0:
            tile = candidate
    return tile if size % tile == 0 else size


def column_parts(width):
    right = width // 2 if width % 512 == 0 else 128
    return [(0, width - right), (width - right, right)]


def column_tile(start, width, most=256):
    for tile in (512, 256, 128):
        if tile <= most and start % tile == 0 and width % tile == 0:
            return tile
    raise ValueError("columns")


NO_COST = pl.CostEstimate(flops=0, bytes_accessed=0, transcendentals=0)


def gates(arrays, *after):
    count = len(arrays)
    return pl.pallas_call(
        lambda *refs: None,
        in_specs=[ANYWHERE] * (count + len(after)),
        out_specs=[ANYWHERE] * count,
        out_shape=[jax.ShapeDtypeStruct(x.shape, x.dtype) for x in arrays],
        input_output_aliases={i: i for i in range(count)},
        compiler_params=vmem(1),
        cost_estimate=NO_COST,
        name="gates",
    )(*arrays, *after)


def gate(x, *after):
    return gates([x], *after)[0]


def copy_gate(x, after):
    def kernel(x_ref, after_ref, out_ref):
        out_ref[...] = x_ref[...]

    return pl.pallas_call(
        kernel,
        in_specs=[pl.BlockSpec(memory_space=pltpu.VMEM), ANYWHERE],
        out_specs=pl.BlockSpec(memory_space=pltpu.VMEM),
        out_shape=jax.ShapeDtypeStruct(x.shape, x.dtype),
        compiler_params=vmem(2),
        cost_estimate=NO_COST,
        name="copy_gate",
    )(x, after)


def chunk_dot(blocks, basis, start, width, after, upper):
    rows, depth = blocks[0].shape
    tokens = rows * len(blocks)
    tile = column_tile(start, width)
    first = start // tile
    count = len(blocks)

    def kernel(upper_ref, *rest):
        block_refs, basis_ref = rest[:count], rest[count]
        keep_ref, send_ref, joint = rest[-3:]

        @pl.when(pl.program_id(0) == 0)
        def _():
            for i, block_ref in enumerate(block_refs):
                joint[i * rows : (i + 1) * rows, :] = block_ref[...]

        total = jnp.dot(joint[...], basis_ref[...], preferred_element_type=F32)
        total = total.astype(BF16)
        half = tokens // 2
        is_upper = upper_ref[0] != 0
        keep_ref[...] = jnp.where(is_upper, total[half:], total[:half])
        send_ref[...] = jnp.where(is_upper, total[:half], total[half:])

    out_rows = tokens // 2
    return pl.pallas_call(
        kernel,
        grid_spec=pltpu.PrefetchScalarGridSpec(
            num_scalar_prefetch=1,
            grid=(width // tile,),
            in_specs=[IN_VMEM] * count
            + [pl.BlockSpec((depth, tile), lambda n, s: (0, first + n))]
            + [ANYWHERE] * len(after),
            out_specs=[pl.BlockSpec((out_rows, tile), lambda n, s: (0, n))] * 2,
            scratch_shapes=[pltpu.VMEM((tokens, depth), BF16)],
        ),
        out_shape=[jax.ShapeDtypeStruct((out_rows, width), BF16)] * 2,
        compiler_params=vmem(16),
        cost_estimate=pl.CostEstimate(
            flops=2 * tokens * depth * width,
            bytes_accessed=2 * depth * width,
            transcendentals=0,
        ),
        name="chunk_dot",
    )(jnp.reshape(upper, (1,)), *blocks, basis, *after)


def first_chunk_dot(blocks, basis, start, width, after, upper):
    part = jnp.dot(
        gate(jnp.concatenate(blocks, axis=0), *after),
        basis[:, start : start + width],
        preferred_element_type=F32,
    )
    return halves(part.astype(BF16), upper != 0)


def lambda_product(place, own, sib, parts, unit, start, width, whole, so_far=None):
    out_rows, seq_tokens = own.shape
    tile_o = largest_tile(out_rows, 128, 256)
    tile_n = min(512, width)
    at_block = start // width
    count = len(parts)
    given = [] if so_far is None else [so_far]

    def kernel(place_ref, own_ref, sib_ref, *rest):
        part_refs, out_ref, acts = rest[:count], rest[-2], rest[-1]

        @pl.when(pl.program_id(0) == 0)
        def _():
            at = 0
            for part in part_refs:
                for h in range(part.shape[0] // unit):
                    rows = pl.ds(pl.multiple_of(place_ref[at] * unit, unit), unit)
                    acts[rows, :] = part[h * unit : (h + 1) * unit, :]
                    at += 1

        for n in range(0, width, tile_n):
            cols = pl.ds(n, min(tile_n, width - n))
            first = jnp.dot(own_ref[...], acts[:seq_tokens, cols], preferred_element_type=F32)
            second = jnp.dot(sib_ref[...], acts[seq_tokens:, cols], preferred_element_type=F32)
            mean = (first * first + second * second) * (1.0 / SEQS)
            out_ref[:, cols] = mean.astype(BF16)

    return pl.pallas_call(
        kernel,
        grid_spec=pltpu.PrefetchScalarGridSpec(
            num_scalar_prefetch=1,
            grid=(out_rows // tile_o,),
            in_specs=[pl.BlockSpec((tile_o, seq_tokens), lambda o, s: (o, 0))] * 2
            + [IN_VMEM] * count
            + [ANYWHERE] * len(given),
            out_specs=pl.BlockSpec((tile_o, width), lambda o, s: (o, at_block)),
            scratch_shapes=[pltpu.VMEM((SEQS * seq_tokens, width), BF16)],
        ),
        out_shape=jax.ShapeDtypeStruct((out_rows, whole), BF16),
        input_output_aliases={3 + count: 0} if given else {},
        compiler_params=vmem(12),
        cost_estimate=pl.CostEstimate(
            flops=2 * out_rows * width * SEQS * seq_tokens,
            bytes_accessed=2 * out_rows * width,
            transcendentals=0,
        ),
        name="lambda_product",
    )(place, own, sib, *parts, *given)


def chip_ring(chips):
    order = list(range(1, chips, 2))
    order = [0] + order + [c for c in range(chips - 1, 0, -1) if c % 2 == 0]
    return {order[i]: order[(i + 1) % chips] for i in range(chips)}


def on_both_cores(pairs):
    return [(CORES * a + k, CORES * b + k) for a, b in pairs for k in range(CORES)]


def powers(n):
    return [1 << b for b in range(n.bit_length() - 1)]


def halves(x, upper):
    half = x.shape[0] // 2
    low, high = x[:half], x[half:]
    return jnp.where(upper, high, low), jnp.where(upper, low, high)


def joined(mine, theirs, upper):
    return jnp.where(
        upper,
        jnp.concatenate([theirs, mine], axis=0),
        jnp.concatenate([mine, theirs], axis=0),
    )


def local(rows_n, cols_n, activations, act_basis, out_grads, grad_basis):
    chips = cols_n // CORES
    col = lax.axis_index("col")
    row = lax.axis_index("row")
    core = col & 1
    swap = lambda x: lax.ppermute(x, "col", [(c, c ^ 1) for c in range(cols_n)])
    trade = lambda x, bit: lax.ppermute(x, "row", [(r, r ^ bit) for r in range(rows_n)])
    bits = powers(rows_n)

    succ = chip_ring(chips)
    pred = {b: a for a, b in succ.items()}
    ring = on_both_cores(sorted(succ.items()))
    blocks = [activations]
    pairs = [(activations, swap(activations))]
    grads = copy_gate(out_grads, pairs[0][1])
    pieces = [grads] + [trade(grads, mask) for mask in range(1, rows_n)]
    for bit in bits:
        pieces = [
            joined(low, high, (row & bit) != 0)
            for low, high in zip(pieces[::2], pieces[1::2])
        ]
    grads = pieces[0]
    for s in range(1, chips):
        block = lax.ppermute(blocks[-1], "col", ring)
        if s == 1:
            block = gate(block, grads)
        blocks.append(block)
        pairs.append((block, swap(block)))

    chip_bits = powers(chips)
    chip_trade = lambda x, bit: lax.ppermute(
        x, "col", on_both_cores([(c, c ^ bit) for c in range(chips)])
    )
    upper_chip = (col & CORES) != 0
    plus = lambda a, b: (a.astype(F32) + b.astype(F32)).astype(BF16)

    def plus_others(x, got, others):
        x = plus(x, got)
        for bit in others[1:]:
            x = plus(x, trade(x, bit))
        return x

    half = chips // 2
    width = act_basis.shape[1]
    (start_l, wide_l), (start_r, wide_r) = column_parts(width)
    early = [b for p in pairs[:half] for b in p]
    late = [b for p in pairs[half:] for b in p]

    part = lax.dot_general(
        grad_basis,
        grads,
        (((0,), (1,)), ((), ())),
        preferred_element_type=F32,
    )
    seq_tokens = part.shape[1] // SEQS
    seqs = [part[:, :seq_tokens], part[:, seq_tokens:]]
    mine = jnp.where(core == 0, seqs[0], seqs[1])
    theirs = jnp.where(core == 0, seqs[1], seqs[0]).astype(BF16)
    mine = mine + swap(theirs).astype(F32)
    mine, away = halves(mine, upper_chip)

    early_bit, early_bits = bits[-1], bits[:-1]
    late_bit, late_bits = bits[0], bits[1:]
    early_upper, late_upper = row & early_bit, row & late_bit
    keep_l, send_l = first_chunk_dot(
        early, act_basis, start_l, wide_l, [theirs], early_upper
    )
    got_l = trade(send_l, early_bit)
    keep_r, send_r = chunk_dot(
        early, act_basis, start_r, wide_r, [blocks[half], send_l], early_upper
    )

    keep_l = plus(keep_l, got_l)
    send_r, keep_l, away = gates([send_r, keep_l, away.astype(BF16)])
    got_r = trade(send_r, early_bit)
    got_l = trade(keep_l, early_bits[0])
    got_away = chip_trade(away, 1)
    late_l, send_l = chunk_dot(late, act_basis, start_l, wide_l, [send_r], late_upper)

    got_r, got_l, got_away = gates([got_r, got_l, got_away], send_l)
    mine = mine + got_away.astype(F32)
    early_l = plus_others(keep_l, got_l, early_bits)
    keep_r = plus(keep_r, got_r)
    send_l, early_l, keep_r, away = gates([send_l, early_l, keep_r, mine.astype(BF16)])
    got_l = trade(send_l, late_bit)
    got_r = trade(keep_r, early_bits[0])
    early_other_l = trade(early_l, early_bit)
    for bit in chip_bits[1:]:
        mine = mine + chip_trade(away, bit).astype(F32)
        away = mine.astype(BF16)
    late_r, send_r = chunk_dot(late, act_basis, start_r, wide_r, [send_l], late_upper)

    got_r, got_l = gates([got_r, got_l], send_r, early_other_l)
    early_r = plus_others(keep_r, got_r, early_bits)
    send_r, late_l, early_r = gates([send_r, plus(late_l, got_l), early_r])
    got_r = trade(send_r, late_bit)
    got_l = trade(late_l, late_bits[0])

    late_l = plus_others(late_l, got_l, late_bits)
    late_l, late_r, own = gates([late_l, plus(late_r, got_r), away])
    late_other_l = trade(late_l, late_bit)
    got_r = trade(late_r, late_bits[0])
    other_own = chip_trade(own, 1)

    late_r = plus_others(late_r, got_r, late_bits)
    own = joined(own, other_own, upper_chip)
    late_r, early_r, own = gates([late_r, early_r, own], late_other_l)
    late_other_r = trade(late_r, late_bit)
    early_other_r = trade(early_r, early_bit)
    sib = swap(own)

    table = []
    for r in range(rows_n):
        for c in range(cols_n):
            here, k = c // CORES, c % CORES
            place = []
            for _ in range(chips):
                block = (here + k * (chips // SEQS)) % chips
                place += [CORES * block + k, CORES * block + 1 - k]
                here = pred[here]
            flat = []
            for at, bit in ((0, early_bit), (chips, late_bit)):
                low, high = place[at : at + half], place[at + half : at + chips]
                flat += high + low if r & bit else low + high
            table.append(flat)
    place = jnp.asarray(np.array(table, np.int32))
    place = lax.dynamic_index_in_dim(place, row * cols_n + col, 0, keepdims=False)
    unit = activations.shape[0]
    parts_l = [early_l, early_other_l, late_l, late_other_l]
    out = lambda_product(place, own, sib, parts_l, unit, start_l, wide_l, width)
    parts_r = [early_r, early_other_r, late_r, late_other_r]
    return lambda_product(place, own, sib, parts_r, unit, start_r, wide_r, width, out)


def solution(mesh):
    rows_n, cols_n = mesh.shape["row"], mesh.shape["col"]

    def body(activations, act_basis, out_grads, grad_basis):
        return local(rows_n, cols_n, activations, act_basis, out_grads, grad_basis)

    return jax.shard_map(
        body,
        mesh=mesh,
        in_specs=(P("col", "row"), P("row", "col"), P("row", "col"), P("col", "row")),
        out_specs=P("row", "col"),
        check_vma=False,
    )
```

profile of v0, /device:TPU:0, one launch (start us, length us, event | category | flops | bytes accessed | tf_op | source)
XLA Modules:
  0.0 160.0 jit_solution(11586213901945222136)
XLA Ops:
  0.5 2.6 %collective-permute-start = (bf16[64,7168]{1,0:T(8,128)(2,1)}, bf16[64,7168]{1,0:T(8,128)(2,1)S(1)}, u32[]{:S(2)}, u32[]{:S(2)}) collective-permute-start(bf16[64,7168]{1,0:T(8,128)(2,1)} %rest_0_.1), channel_id=1, source_target_pairs={{0,2},{1,3},{2,6},{3,7},{4,0},{5,1},{6,4},{7,5},{8,10},{9,11},{10,... | collective-permute-start | bytes 2752520 | tf_op jit(solution)/shard_map/ppermute | solution.py:235
  4.0 2.7 %collective-permute-start.4 = (bf16[128,1024]{1,0:T(8,128)(2,1)S(1)}, bf16[128,1024]{1,0:T(8,128)(2,1)S(1)}, u32[]{:S(2)}, u32[]{:S(2)}) collective-permute-start(bf16[128,1024]{1,0:T(8,128)(2,1)S(1)} %copy_gate.1), channel_id=1, source_target_pairs={{0,8},{8,0},{16,24},{24,16},{1,9},{9,1},{17,25},{25,17},{2,10},{10... | collective-permute-start | bytes 786440 | tf_op jit(solution)/shard_map/ppermute | solution.py:218
  8.2 5.5 %collective-permute-done.4 = bf16[128,1024]{1,0:T(8,128)(2,1)S(1)} collective-permute-done((bf16[128,1024]{1,0:T(8,128)(2,1)S(1)}, bf16[128,1024]{1,0:T(8,128)(2,1)S(1)}, u32[]{:S(2)}, u32[]{:S(2)}) %collective-permute-start.4) | collective-permute-done | bytes 262176 | tf_op jit(solution)/shard_map/ppermute | solution.py:218
  13.9 6.5 %collective-permute-done.3 = bf16[128,1024]{1,0:T(8,128)(2,1)S(1)} collective-permute-done((bf16[128,1024]{1,0:T(8,128)(2,1)S(1)}, bf16[128,1024]{1,0:T(8,128)(2,1)S(1)}, u32[]{:S(2)}, u32[]{:S(2)}) %collective-permute-start.3) | collective-permute-done | bytes 262176 | tf_op jit(solution)/shard_map/ppermute | solution.py:218
  21.0 4.3 %collective-permute-done.refs_0_ = bf16[64,7168]{1,0:T(8,128)(2,1)S(1)} collective-permute-done((bf16[64,7168]{1,0:T(8,128)(2,1)}, bf16[64,7168]{1,0:T(8,128)(2,1)S(1)}, u32[]{:S(2)}, u32[]{:S(2)}) %collective-permute-start) | collective-permute-done | bytes 917536 | tf_op jit(solution)/shard_map/ppermute | solution.py:235
  26.2 2.4 %convolution_bitcast_fusion = f32[2048,512]{1,0:T(8,128)S(1)} fusion(bf16[512,1024]{1,0:T(8,128)(2,1)S(1)} %maximum_select_fusion.refs_1_, bf16[1024,2048]{1,0:T(8,128)(2,1)S(1)} %copy-done.10), kind=kOutput, calls=%fused_computation.3 | convolution fusion | flops 2147483648 | bytes 9437184 | tf_op jit(solution)/shard_map/dot_general | solution.py:260
  30.8 11.5 %fusion.2 = bf16[256,1792]{1,0:T(8,128)(2,1)S(1)} fusion(bf16[256,7168]{1,0:T(8,128)(2,1)S(1)} %gates.10, bf16[7168,3584]{1,0:T(8,128)(2,1)} %rest_4_.5), kind=kOutput, calls=%fused_computation.4 | convolution fusion | flops 6577127424 | bytes 30277632 | tf_op jit(solution)/shard_map/dot_general | solution.py:126
  42.3 6.6 %collective-permute-done.5.rest_5_.rest_0_ = bf16[64,7168]{1,0:T(8,128)(2,1)S(1)} collective-permute-done((bf16[64,7168]{1,0:T(8,128)(2,1)S(1)}, bf16[64,7168]{1,0:T(8,128)(2,1)S(1)}, u32[]{:S(2)}, u32[]{:S(2)}) %collective-permute-start.5) | collective-permute-done | bytes 917536 | tf_op jit(solution)/shard_map/ppermute | solution.py:235
  49.8 1.6 collective-permute-start.10
  51.4 13.3 %chunk_dot.3 = (bf16[128,1792]{1,0:T(8,128)(2,1)S(1)}, bf16[128,1792]{1,0:T(8,128)(2,1)S(1)}) custom-call(s32[1]{0:T(128)} %bitcast.2.upper_ref, bf16[64,7168]{1,0:T(8,128)(2,1)S(1)} %copy-done.2, bf16[64,7168]{1,0:T(8,128)(2,1)S(1)} %collective-permute-done.1.after_ref.rest_1_, bf16[64,7168]{1,0:T(8,128)(2,1)S(1)} %gates.9.rest_2_, ...), custom_call_target="tpu_custom_call" | custom-call | flops 6576668672 | bytes 25690112 | tf_op jit(solution)/shard_map/chunk_dot/pallas_call | solution.py:103
  64.7 7.1 %collective-permute-done.7.rest_2_ = bf16[64,7168]{1,0:T(8,128)(2,1)S(1)} collective-permute-done((bf16[64,7168]{1,0:T(8,128)(2,1)S(1)}, bf16[64,7168]{1,0:T(8,128)(2,1)S(1)}, u32[]{:S(2)}, u32[]{:S(2)}) %collective-permute-start.7) | collective-permute-done | bytes 917536 | tf_op jit(solution)/shard_map/ppermute | solution.py:235
  71.8 1.6 %convert_add_fusion = f32[2048,256]{1,0:T(8,128)S(1)} fusion(bf16[2048,256]{1,0:T(8,128)(2,1)} %collective-permute-done.11, f32[2048,512]{1,0:T(8,128)S(1)} %copy-done.9, pred[]{:T(512)S(6)} %eq.4), kind=kLoop, calls=%fused_computation.5 | loop fusion | flops 1572864 | bytes 7340033 | tf_op jit(solution)/shard_map/add | solution.py:270
  73.8 1.6 %collective-permute-start.12 = (bf16[128,1792]{1,0:T(8,128)(2,1)S(1)}, bf16[128,1792]{1,0:T(8,128)(2,1)S(1)}, u32[]{:S(2)}, u32[]{:S(2)}) collective-permute-start(bf16[128,1792]{1,0:T(8,128)(2,1)S(1)} %get-tuple-element.33.rest_5_), channel_id=1, source_target_pairs={{0,16},{8,24},{16,0},{24,8},{1,17},{9,25},{17,1},{25,9},{2,18},{10... | collective-permute-start | bytes 1376264 | tf_op jit(solution)/shard_map/ppermute | solution.py:218
  77.7 13.1 %chunk_dot.4 = (bf16[128,1792]{1,0:T(8,128)(2,1)S(1)}, bf16[128,1792]{1,0:T(8,128)(2,1)S(1)}) custom-call(s32[1]{0:T(128)} %bitcast.1.upper_ref, bf16[64,7168]{1,0:T(8,128)(2,1)S(1)} %collective-permute-done.5.rest_5_.rest_0_, bf16[64,7168]{1,0:T(8,128)(2,1)S(1)} %collective-permute-done.6.rest_1_, bf16[64,7168]{1,0:T(8,128)(2,1)S(1)} %collective-permute-done.7.rest_2_, ...), custom_call_target="tpu_custom_call" | custom-call | flops 6576668672 | bytes 25690112 | tf_op jit(solution)/shard_map/chunk_dot/pallas_call | solution.py:103
  93.9 3.4 %collective-permute-start.20 = (bf16[1024,256]{1,0:T(8,128)(2,1)S(1)}, bf16[1024,256]{1,0:T(8,128)(2,1)S(1)}, u32[]{:S(2)}, u32[]{:S(2)}) collective-permute-start(bf16[1024,256]{1,0:T(8,128)(2,1)S(1)} %get-tuple-element.51), channel_id=1, source_target_pairs={{0,4},{1,5},{2,6},{3,7},{4,0},{5,1},{6,2},{7,3},{8,12},{9,13},{10,... | collective-permute-start | bytes 1572872 | tf_op jit(solution)/shard_map/ppermute | solution.py:242
  97.3 13.2 %chunk_dot.5 = (bf16[128,1792]{1,0:T(8,128)(2,1)S(1)}, bf16[128,1792]{1,0:T(8,128)(2,1)S(1)}) custom-call(s32[1]{0:T(128)} %bitcast.1.upper_ref, bf16[64,7168]{1,0:T(8,128)(2,1)S(1)} %collective-permute-done.5.rest_5_.rest_0_, bf16[64,7168]{1,0:T(8,128)(2,1)S(1)} %collective-permute-done.6.rest_1_, bf16[64,7168]{1,0:T(8,128)(2,1)S(1)} %collective-permute-done.7.rest_2_, ...), custom_call_target="tpu_custom_call" | custom-call | flops 6576668672 | bytes 25690112 | tf_op jit(solution)/shard_map/chunk_dot/pallas_call | solution.py:103
  110.5 2.7 %collective-permute-done.15.refs_0_ = bf16[128,1792]{1,0:T(8,128)(2,1)S(1)} collective-permute-done((bf16[128,1792]{1,0:T(8,128)(2,1)S(1)}, bf16[128,1792]{1,0:T(8,128)(2,1)S(1)}, u32[]{:S(2)}, u32[]{:S(2)}) %collective-permute-start.15) | collective-permute-done | bytes 458784 | tf_op jit(solution)/shard_map/ppermute | solution.py:218
  114.7 4.7 %collective-permute-done.20 = bf16[1024,256]{1,0:T(8,128)(2,1)S(1)} collective-permute-done((bf16[1024,256]{1,0:T(8,128)(2,1)S(1)}, bf16[1024,256]{1,0:T(8,128)(2,1)S(1)}, u32[]{:S(2)}, u32[]{:S(2)}) %collective-permute-start.20) | collective-permute-done | bytes 524320 | tf_op jit(solution)/shard_map/ppermute | solution.py:242
  119.6 5.2 %collective-permute-done.18 = bf16[128,1792]{1,0:T(8,128)(2,1)S(1)} collective-permute-done((bf16[128,1792]{1,0:T(8,128)(2,1)S(1)}, bf16[128,1792]{1,0:T(8,128)(2,1)S(1)}, u32[]{:S(2)}, u32[]{:S(2)}) %collective-permute-start.18) | collective-permute-done | bytes 458784 | tf_op jit(solution)/shard_map/ppermute | solution.py:218
  125.2 1.6 collective-permute-start.21
  128.5 6.9 %collective-permute-done.21 = bf16[128,1792]{1,0:T(8,128)(2,1)S(1)} collective-permute-done((bf16[128,1792]{1,0:T(8,128)(2,1)S(1)}, bf16[128,1792]{1,0:T(8,128)(2,1)S(1)}, u32[]{:S(2)}, u32[]{:S(2)}) %collective-permute-start.21) | collective-permute-done | bytes 458784 | tf_op jit(solution)/shard_map/ppermute | solution.py:218
  135.5 2.4 %collective-permute-done.22 = bf16[1024,256]{1,0:T(8,128)(2,1)S(1)} collective-permute-done((bf16[1024,256]{1,0:T(8,128)(2,1)S(1)}, bf16[1024,256]{1,0:T(8,128)(2,1)S(1)}, u32[]{:S(2)}, u32[]{:S(2)}) %collective-permute-start.22) | collective-permute-done | bytes 524320 | tf_op jit(solution)/shard_map/ppermute | solution.py:242
  144.7 7.7 %lambda_product.2.rest_4_ = bf16[2048,3584]{1,0:T(8,128)(2,1)} custom-call(s32[8]{0:T(128)S(1)} %dynamic-slice_bitcast_fusion.place_ref, bf16[2048,256]{1,0:T(8,128)(2,1)S(1)} %get-tuple-element.56.own_ref, bf16[2048,256]{1,0:T(8,128)(2,1)S(1)} %collective-permute-done.24.sib_ref, bf16[128,1792]{1,0:T(8,128)(2,1)S(1)} %copy-done.1, ...), custom_call_target="tpu_custom_call" | custom-call | flops 3758096384 | bytes 7340032 | tf_op jit(solution)/shard_map/lambda_product/pallas_call | solution.py:161
  152.3 7.7 %lambda_product.3 = bf16[2048,3584]{1,0:T(8,128)(2,1)} custom-call(s32[8]{0:T(128)S(1)} %dynamic-slice_bitcast_fusion.place_ref, bf16[2048,256]{1,0:T(8,128)(2,1)S(1)} %get-tuple-element.56.own_ref, bf16[2048,256]{1,0:T(8,128)(2,1)S(1)} %collective-permute-done.24.sib_ref, ...), custom_call_target="tpu_custom_call", output_to_operand_aliasing={{}: (7, {})} | custom-call | flops 3758096384 | bytes 7340032 | tf_op jit(solution)/shard_map/lambda_product/pallas_call | solution.py:161
  (88 shorter events, 23.9 us)
Async XLA Ops:
  0.5 24.8 %collective-permute-start = (bf16[64,7168]{1,0:T(8,128)(2,1)}, bf16[64,7168]{1,0:T(8,128)(2,1)S(1)}, u32[]{:S(2)}, u32[]{:S(2)}) collective-permute-start(bf16[64,7168]{1,0:T(8,128)(2,1)} %rest_0_.1), channel_id=1, source_target_pairs={{0,2},{1,3},{2,6},{3,7},{4,0},{5,1},{6,4},{7,5},{8,10},{9,11},{10,... | collective-permute-start | bytes 2752520 | tf_op jit(solution)/shard_map/ppermute | solution.py:235
  4.0 9.7 %collective-permute-start.4 = (bf16[128,1024]{1,0:T(8,128)(2,1)S(1)}, bf16[128,1024]{1,0:T(8,128)(2,1)S(1)}, u32[]{:S(2)}, u32[]{:S(2)}) collective-permute-start(bf16[128,1024]{1,0:T(8,128)(2,1)S(1)} %copy_gate.1), channel_id=1, source_target_pairs={{0,8},{8,0},{16,24},{24,16},{1,9},{9,1},{17,25},{25,17},{2,10},{10... | collective-permute-start | bytes 786440 | tf_op jit(solution)/shard_map/ppermute | solution.py:218
  6.7 13.7 %collective-permute-start.3 = (bf16[128,1024]{1,0:T(8,128)(2,1)S(1)}, bf16[128,1024]{1,0:T(8,128)(2,1)S(1)}, u32[]{:S(2)}, u32[]{:S(2)}) collective-permute-start(bf16[128,1024]{1,0:T(8,128)(2,1)S(1)} %copy_gate.1), channel_id=1, source_target_pairs={{0,16},{8,24},{16,0},{24,8},{1,17},{9,25},{17,1},{25,9},{2,18},{10... | collective-permute-start | bytes 786440 | tf_op jit(solution)/shard_map/ppermute | solution.py:218
  8.2 12.2 %collective-permute-start.2 = (bf16[128,1024]{1,0:T(8,128)(2,1)S(1)}, bf16[128,1024]{1,0:T(8,128)(2,1)S(1)}, u32[]{:S(2)}, u32[]{:S(2)}) collective-permute-start(bf16[128,1024]{1,0:T(8,128)(2,1)S(1)} %copy_gate.1), channel_id=1, source_target_pairs={{0,24},{8,16},{16,8},{24,0},{1,25},{9,17},{17,9},{25,1},{2,26},{10... | collective-permute-start | bytes 786440 | tf_op jit(solution)/shard_map/ppermute | solution.py:218
  25.3 23.7 %collective-permute-start.5 = (bf16[64,7168]{1,0:T(8,128)(2,1)S(1)}, bf16[64,7168]{1,0:T(8,128)(2,1)S(1)}, u32[]{:S(2)}, u32[]{:S(2)}) collective-permute-start(bf16[64,7168]{1,0:T(8,128)(2,1)S(1)} %gates.9.rest_2_), channel_id=1, source_target_pairs={{0,2},{1,3},{2,6},{3,7},{4,0},{5,1},{6,4},{7,5},{8,10},{9,11},{10,... | collective-permute-start | bytes 2752520 | tf_op jit(solution)/shard_map/ppermute | solution.py:235
  28.8 43.0 %collective-permute-start.11 = (bf16[2048,256]{1,0:T(8,128)(2,1)S(1)}, bf16[2048,256]{1,0:T(8,128)(2,1)}, u32[]{:S(2)}, u32[]{:S(2)}) collective-permute-start(bf16[2048,256]{1,0:T(8,128)(2,1)S(1)} %select_convert_fusion.refs_1_), channel_id=1, source_target_pairs={{0,1},{1,0},{2,3},{3,2},{4,5},{5,4},{6,7},{7,6},{8,9},{9,8},{10,11... | collective-permute-start | bytes 3145736 | tf_op jit(solution)/shard_map/ppermute | solution.py:217
  48.9 22.9 %collective-permute-start.7 = (bf16[64,7168]{1,0:T(8,128)(2,1)S(1)}, bf16[64,7168]{1,0:T(8,128)(2,1)S(1)}, u32[]{:S(2)}, u32[]{:S(2)}) collective-permute-start(bf16[64,7168]{1,0:T(8,128)(2,1)S(1)} %collective-permute-done.5.rest_5_.rest_0_), channel_id=1, source_target_pairs={{0,2},{1,3},{2,6},{3,7},{4,0},{5,1},{6,4},{7,5},{8,10},{9,11},{10,... | collective-permute-start | bytes 2752520 | tf_op jit(solution)/shard_map/ppermute | solution.py:235
  49.8 23.7 %collective-permute-start.10 = (bf16[128,1792]{1,0:T(8,128)(2,1)S(1)}, bf16[128,1792]{1,0:T(8,128)(2,1)S(1)}, u32[]{:S(2)}, u32[]{:S(2)}) collective-permute-start(bf16[128,1792]{1,0:T(8,128)(2,1)S(1)} %broadcast_select_fusion.rest_6_), channel_id=1, source_target_pairs={{0,16},{8,24},{16,0},{24,8},{1,17},{9,25},{17,1},{25,9},{2,18},{10... | collective-permute-start | bytes 1376264 | tf_op jit(solution)/shard_map/ppermute | solution.py:218
  51.4 26.3 %collective-permute-start.6 = (bf16[64,7168]{1,0:T(8,128)(2,1)S(1)}, bf16[64,7168]{1,0:T(8,128)(2,1)S(1)}, u32[]{:S(2)}, u32[]{:S(2)}) collective-permute-start(bf16[64,7168]{1,0:T(8,128)(2,1)S(1)} %collective-permute-done.5.rest_5_.rest_0_), channel_id=1, source_target_pairs={{0,1},{1,0},{2,3},{3,2},{4,5},{5,4},{6,7},{7,6},{8,9},{9,8},{10,11... | collective-permute-start | bytes 2752520 | tf_op jit(solution)/shard_map/ppermute | solution.py:217
  71.8 5.9 %collective-permute-start.8 = (bf16[64,7168]{1,0:T(8,128)(2,1)S(1)}, bf16[64,7168]{1,0:T(8,128)(2,1)S(1)}, u32[]{:S(2)}, u32[]{:S(2)}) collective-permute-start(bf16[64,7168]{1,0:T(8,128)(2,1)S(1)} %collective-permute-done.7.rest_2_), channel_id=1, source_target_pairs={{0,1},{1,0},{2,3},{3,2},{4,5},{5,4},{6,7},{7,6},{8,9},{9,8},{10,11... | collective-permute-start | bytes 2752520 | tf_op jit(solution)/shard_map/ppermute | solution.py:217
  73.8 17.0 %collective-permute-start.12 = (bf16[128,1792]{1,0:T(8,128)(2,1)S(1)}, bf16[128,1792]{1,0:T(8,128)(2,1)S(1)}, u32[]{:S(2)}, u32[]{:S(2)}) collective-permute-start(bf16[128,1792]{1,0:T(8,128)(2,1)S(1)} %get-tuple-element.33.rest_5_), channel_id=1, source_target_pairs={{0,16},{8,24},{16,0},{24,8},{1,17},{9,25},{17,1},{25,9},{2,18},{10... | collective-permute-start | bytes 1376264 | tf_op jit(solution)/shard_map/ppermute | solution.py:218
  75.4 15.4 %collective-permute-start.13 = (bf16[128,1792]{1,0:T(8,128)(2,1)S(1)}, bf16[128,1792]{1,0:T(8,128)(2,1)S(1)}, u32[]{:S(2)}, u32[]{:S(2)}) collective-permute-start(bf16[128,1792]{1,0:T(8,128)(2,1)S(1)} %get-tuple-element.35), channel_id=1, source_target_pairs={{0,8},{8,0},{16,24},{24,16},{1,9},{9,1},{17,25},{25,17},{2,10},{10... | collective-permute-start | bytes 1376264 | tf_op jit(solution)/shard_map/ppermute | solution.py:218
  76.9 13.9 %collective-permute-start.14 = (bf16[1024,256]{1,0:T(8,128)(2,1)S(1)}, bf16[1024,256]{1,0:T(8,128)(2,1)S(1)}, u32[]{:S(2)}, u32[]{:S(2)}) collective-permute-start(bf16[1024,256]{1,0:T(8,128)(2,1)S(1)} %get-tuple-element.36), channel_id=1, source_target_pairs={{0,2},{1,3},{2,0},{3,1},{4,6},{5,7},{6,4},{7,5},{8,10},{9,11},{10,... | collective-permute-start | bytes 1572872 | tf_op jit(solution)/shard_map/ppermute | solution.py:242
  91.3 19.2 %collective-permute-start.16 = (bf16[128,1792]{1,0:T(8,128)(2,1)S(1)}, bf16[128,1792]{1,0:T(8,128)(2,1)S(1)}, u32[]{:S(2)}, u32[]{:S(2)}) collective-permute-start(bf16[128,1792]{1,0:T(8,128)(2,1)S(1)} %get-tuple-element.41.rest_5_), channel_id=1, source_target_pairs={{0,8},{8,0},{16,24},{24,16},{1,9},{9,1},{17,25},{25,17},{2,10},{10... | collective-permute-start | bytes 1376264 | tf_op jit(solution)/shard_map/ppermute | solution.py:218
  91.9 21.4 %collective-permute-start.15 = (bf16[128,1792]{1,0:T(8,128)(2,1)S(1)}, bf16[128,1792]{1,0:T(8,128)(2,1)S(1)}, u32[]{:S(2)}, u32[]{:S(2)}) collective-permute-start(bf16[128,1792]{1,0:T(8,128)(2,1)S(1)} %get-tuple-element.44), channel_id=1, source_target_pairs={{0,8},{8,0},{16,24},{24,16},{1,9},{9,1},{17,25},{25,17},{2,10},{10... | collective-permute-start | bytes 1376264 | tf_op jit(solution)/shard_map/ppermute | solution.py:218
  93.4 19.9 %collective-permute-start.17 = (bf16[128,1792]{1,0:T(8,128)(2,1)S(1)}, bf16[128,1792]{1,0:T(8,128)(2,1)S(1)}, u32[]{:S(2)}, u32[]{:S(2)}) collective-permute-start(bf16[128,1792]{1,0:T(8,128)(2,1)S(1)} %get-tuple-element.45.rest_0_), channel_id=1, source_target_pairs={{0,16},{8,24},{16,0},{24,8},{1,17},{9,25},{17,1},{25,9},{2,18},{10... | collective-permute-start | bytes 1376264 | tf_op jit(solution)/shard_map/ppermute | solution.py:218
  93.9 25.5 %collective-permute-start.20 = (bf16[1024,256]{1,0:T(8,128)(2,1)S(1)}, bf16[1024,256]{1,0:T(8,128)(2,1)S(1)}, u32[]{:S(2)}, u32[]{:S(2)}) collective-permute-start(bf16[1024,256]{1,0:T(8,128)(2,1)S(1)} %get-tuple-element.51), channel_id=1, source_target_pairs={{0,4},{1,5},{2,6},{3,7},{4,0},{5,1},{6,2},{7,3},{8,12},{9,13},{10,... | collective-permute-start | bytes 1572872 | tf_op jit(solution)/shard_map/ppermute | solution.py:242
  113.6 11.3 %collective-permute-start.18 = (bf16[128,1792]{1,0:T(8,128)(2,1)S(1)}, bf16[128,1792]{1,0:T(8,128)(2,1)S(1)}, u32[]{:S(2)}, u32[]{:S(2)}) collective-permute-start(bf16[128,1792]{1,0:T(8,128)(2,1)S(1)} %get-tuple-element.48), channel_id=1, source_target_pairs={{0,16},{8,24},{16,0},{24,8},{1,17},{9,25},{17,1},{25,9},{2,18},{10... | collective-permute-start | bytes 1376264 | tf_op jit(solution)/shard_map/ppermute | solution.py:218
  114.1 10.9 %collective-permute-start.19 = (bf16[128,1792]{1,0:T(8,128)(2,1)S(1)}, bf16[128,1792]{1,0:T(8,128)(2,1)S(1)}, u32[]{:S(2)}, u32[]{:S(2)}) collective-permute-start(bf16[128,1792]{1,0:T(8,128)(2,1)S(1)} %get-tuple-element.50), channel_id=1, source_target_pairs={{0,8},{8,0},{16,24},{24,16},{1,9},{9,1},{17,25},{25,17},{2,10},{10... | collective-permute-start | bytes 1376264 | tf_op jit(solution)/shard_map/ppermute | solution.py:218
  125.2 10.2 %collective-permute-start.21 = (bf16[128,1792]{1,0:T(8,128)(2,1)S(1)}, bf16[128,1792]{1,0:T(8,128)(2,1)S(1)}, u32[]{:S(2)}, u32[]{:S(2)}) collective-permute-start(bf16[128,1792]{1,0:T(8,128)(2,1)S(1)} %get-tuple-element.52), channel_id=1, source_target_pairs={{0,16},{8,24},{16,0},{24,8},{1,17},{9,25},{17,1},{25,9},{2,18},{10... | collective-permute-start | bytes 1376264 | tf_op jit(solution)/shard_map/ppermute | solution.py:218
  126.7 11.1 %collective-permute-start.22 = (bf16[1024,256]{1,0:T(8,128)(2,1)S(1)}, bf16[1024,256]{1,0:T(8,128)(2,1)S(1)}, u32[]{:S(2)}, u32[]{:S(2)}) collective-permute-start(bf16[1024,256]{1,0:T(8,128)(2,1)S(1)} %get-tuple-element.54), channel_id=1, source_target_pairs={{0,2},{1,3},{2,0},{3,1},{4,6},{5,7},{6,4},{7,5},{8,10},{9,11},{10,... | collective-permute-start | bytes 1572872 | tf_op jit(solution)/shard_map/ppermute | solution.py:242
  128.0 10.2 %collective-permute-start.23 = (bf16[128,1792]{1,0:T(8,128)(2,1)S(1)}, bf16[128,1792]{1,0:T(8,128)(2,1)S(1)}, u32[]{:S(2)}, u32[]{:S(2)}) collective-permute-start(bf16[128,1792]{1,0:T(8,128)(2,1)S(1)} %get-tuple-element.55.rest_2_), channel_id=1, source_target_pairs={{0,8},{8,0},{16,24},{24,16},{1,9},{9,1},{17,25},{25,17},{2,10},{10... | collective-permute-start | bytes 1376264 | tf_op jit(solution)/shard_map/ppermute | solution.py:218
  138.9 13.4 %collective-permute-start.25 = (bf16[128,1792]{1,0:T(8,128)(2,1)S(1)}, bf16[128,1792]{1,0:T(8,128)(2,1)S(1)}, u32[]{:S(2)}, u32[]{:S(2)}) collective-permute-start(bf16[128,1792]{1,0:T(8,128)(2,1)S(1)} %get-tuple-element.57.rest_0_), channel_id=1, source_target_pairs={{0,16},{8,24},{16,0},{24,8},{1,17},{9,25},{17,1},{25,9},{2,18},{10... | collective-permute-start | bytes 1376264 | tf_op jit(solution)/shard_map/ppermute | solution.py:218
  139.6 12.7 %collective-permute-start.26 = (bf16[128,1792]{1,0:T(8,128)(2,1)S(1)}, bf16[128,1792]{1,0:T(8,128)(2,1)S(1)}, u32[]{:S(2)}, u32[]{:S(2)}) collective-permute-start(bf16[128,1792]{1,0:T(8,128)(2,1)S(1)} %get-tuple-element.58.rest_2_), channel_id=1, source_target_pairs={{0,8},{8,0},{16,24},{24,16},{1,9},{9,1},{17,25},{25,17},{2,10},{10... | collective-permute-start | bytes 1376264 | tf_op jit(solution)/shard_map/ppermute | solution.py:218
  (14 other events, 77.4 us)
where the time goes:
time: 161 us; the launch traced here: 160 us
  Pallas kernels  55 us (34%)
  waiting for transfers between devices  52.8 us (33%)
  starting transfers between devices  26.5 us (16%)
  matrix products  13.9 us (9%)
  local copies, waits for them, and re-layouts  6.86 us (4%)
  other arithmetic  4.69 us (3%)
    pallas_call x3, Pallas kernels, chunk_dot(): pl.pallas_call(kernel, grid_spec=pltpu.PrefetchScalarGridSpec(num_scalar_...  39.6 us
    ppermute x15, waiting for transfers between devices, local(): lax.ppermute(x, 'row', [(r, r ^ bit) for r in range(rows_n)])  26.9 us
    ppermute x3, waiting for transfers between devices, local(): block = lax.ppermute(blocks[-1], 'col', ring)  18 us
    ppermute x15, starting transfers between devices, local(): lax.ppermute(x, 'row', [(r, r ^ bit) for r in range(rows_n)])  16 us
    pallas_call x2, Pallas kernels, lambda_product(): pl.pallas_call(kernel, grid_spec=pltpu.PrefetchScalarGridSpec(num_scalar_...  15.4 us
    dot_general x1, matrix products, first_chunk_dot(): jnp.dot(gate(jnp.concatenate(blocks, axis=0), *after), basis[:, start:sta...  11.5 us
    ppermute x3, waiting for transfers between devices, local(): lax.ppermute(x, 'col', on_both_cores([(c, c ^ bit) for c in range(chips)]))  7.05 us
    unnamed x22, local copies, waits for them, and re-layouts  6.17 us
  transfers between devices with their start and end apart: 27, of which 12 were waited for; matrix products, arithmetic and copies ran while one was open for 12% of the time, Pallas kernels for 30%

commit v1 on v0

--- a/solution.py
+++ b/solution.py
@@ -112,7 +112,7 @@
             scratch_shapes=[pltpu.VMEM((tokens, depth), BF16)],
         ),
         out_shape=[jax.ShapeDtypeStruct((out_rows, width), BF16)] * 2,
-        compiler_params=vmem(16),
+        compiler_params=vmem(14),
         cost_estimate=pl.CostEstimate(
             flops=2 * tokens * depth * width,
             bytes_accessed=2 * depth * width,
@@ -134,7 +134,7 @@
 def lambda_product(place, own, sib, parts, unit, start, width, whole, so_far=None):
     out_rows, seq_tokens = own.shape
     tile_o = largest_tile(out_rows, 128, 256)
-    tile_n = min(512, width)
+    tile_n = width // 2 if width % 256 == 0 else width
     at_block = start // width
     count = len(parts)
     given = [] if so_far is None else [so_far]
@@ -171,7 +171,7 @@
         ),
         out_shape=jax.ShapeDtypeStruct((out_rows, whole), BF16),
         input_output_aliases={3 + count: 0} if given else {},
-        compiler_params=vmem(12),
+        compiler_params=vmem(8),
         cost_estimate=pl.CostEstimate(
             flops=2 * out_rows * width * SEQS * seq_tokens,
             bytes_accessed=2 * out_rows * width,
@@ -273,53 +273,6 @@
     early_bit, early_bits = bits[-1], bits[:-1]
     late_bit, late_bits = bits[0], bits[1:]
     early_upper, late_upper = row & early_bit, row & late_bit
-    keep_l, send_l = first_chunk_dot(
-        early, act_basis, start_l, wide_l, [theirs], early_upper
-    )
-    got_l = trade(send_l, early_bit)
-    keep_r, send_r = chunk_dot(
-        early, act_basis, start_r, wide_r, [blocks[half], send_l], early_upper
-    )
-
-    keep_l = plus(keep_l, got_l)
-    send_r, keep_l, away = gates([send_r, keep_l, away.astype(BF16)])
-    got_r = trade(send_r, early_bit)
-    got_l = trade(keep_l, early_bits[0])
-    got_away = chip_trade(away, 1)
-    late_l, send_l = chunk_dot(late, act_basis, start_l, wide_l, [send_r], late_upper)
-
-    got_r, got_l, got_away = gates([got_r, got_l, got_away], send_l)
-    mine = mine + got_away.astype(F32)
-    early_l = plus_others(keep_l, got_l, early_bits)
-    keep_r = plus(keep_r, got_r)
-    send_l, early_l, keep_r, away = gates([send_l, early_l, keep_r, mine.astype(BF16)])
-    got_l = trade(send_l, late_bit)
-    got_r = trade(keep_r, early_bits[0])
-    early_other_l = trade(early_l, early_bit)
-    for bit in chip_bits[1:]:
-        mine = mine + chip_trade(away, bit).astype(F32)
-        away = mine.astype(BF16)
-    late_r, send_r = chunk_dot(late, act_basis, start_r, wide_r, [send_l], late_upper)
-
-    got_r, got_l = gates([got_r, got_l], send_r, early_other_l)
-    early_r = plus_others(keep_r, got_r, early_bits)
-    send_r, late_l, early_r = gates([send_r, plus(late_l, got_l), early_r])
-    got_r = trade(send_r, late_bit)
-    got_l = trade(late_l, late_bits[0])
-
-    late_l = plus_others(late_l, got_l, late_bits)
-    late_l, late_r, own = gates([late_l, plus(late_r, got_r), away])
-    late_other_l = trade(late_l, late_bit)
-    got_r = trade(late_r, late_bits[0])
-    other_own = chip_trade(own, 1)
-
-    late_r = plus_others(late_r, got_r, late_bits)
-    own = joined(own, other_own, upper_chip)
-    late_r, early_r, own = gates([late_r, early_r, own], late_other_l)
-    late_other_r = trade(late_r, late_bit)
-    early_other_r = trade(early_r, early_bit)
-    sib = swap(own)
-
     table = []
     for r in range(rows_n):
         for c in range(cols_n):
@@ -336,6 +289,54 @@
             table.append(flat)
     place = jnp.asarray(np.array(table, np.int32))
     place = lax.dynamic_index_in_dim(place, row * cols_n + col, 0, keepdims=False)
+
+    keep_l, send_l = first_chunk_dot(
+        early, act_basis, start_l, wide_l, [theirs, place], early_upper
+    )
+    got_l = trade(send_l, early_bit)
+    keep_r, send_r = chunk_dot(
+        early, act_basis, start_r, wide_r, [blocks[half], send_l], early_upper
+    )
+
+    keep_l = plus(keep_l, got_l)
+    send_r, keep_l, away = gates([send_r, keep_l, away.astype(BF16)])
+    got_r = trade(send_r, early_bit)
+    got_l = trade(keep_l, early_bits[0])
+    got_away = chip_trade(away, 1)
+    late_l, send_l = chunk_dot(late, act_basis, start_l, wide_l, [send_r], late_upper)
+
+    got_r, got_l, got_away = gates([got_r, got_l, got_away], send_l)
+    mine = mine + got_away.astype(F32)
+    early_l = plus_others(keep_l, got_l, early_bits)
+    keep_r = plus(keep_r, got_r)
+    send_l, early_l, keep_r, away = gates([send_l, early_l, keep_r, mine.astype(BF16)])
+    got_l = trade(send_l, late_bit)
+    got_r = trade(keep_r, early_bits[0])
+    early_other_l = trade(early_l, early_bit)
+    for bit in chip_bits[1:]:
+        mine = mine + chip_trade(away, bit).astype(F32)
+        away = mine.astype(BF16)
+    late_r, send_r = chunk_dot(late, act_basis, start_r, wide_r, [send_l], late_upper)
+
+    got_r, got_l = gates([got_r, got_l], send_r, early_other_l)
+    early_r = plus_others(keep_r, got_r, early_bits)
+    send_r, late_l, early_r = gates([send_r, plus(late_l, got_l), early_r])
+    got_r = trade(send_r, late_bit)
+    got_l = trade(late_l, late_bits[0])
+
+    late_l = plus_others(late_l, got_l, late_bits)
+    late_l, late_r = gates([late_l, plus(late_r, got_r)])
+    late_other_l = trade(late_l, late_bit)
+    got_r = trade(late_r, late_bits[0])
+    other_own = chip_trade(away, 1)
+
+    late_r = plus_others(late_r, got_r, late_bits)
+    own = joined(away, other_own, upper_chip)
+    late_r, early_r, own = gates([late_r, early_r, own], late_other_l)
+    late_other_r = trade(late_r, late_bit)
+    early_other_r = trade(early_r, early_bit)
+    sib = swap(own)
+
     unit = activations.shape[0]
     parts_l = [early_l, early_other_l, late_l, late_other_l]
     out = lambda_product(place, own, sib, parts_l, unit, start_l, wide_l, width)

time: 161 us -> 159 us (0.988)
  local copies, waits for them, and re-layouts: 6.86 us -> 3.18 us
  waiting for transfers between devices: 52.8 us -> 54.7 us
    ppermute x3, waiting for transfers between devices: 7.05 us -> 11 us  [local(): lax.ppermute(x, 'col', on_both_cores([(c, c ^ bit) for c in range(chips)]))]
    unnamed x22 -> x10, local copies, waits for them, and re-layouts: 6.17 us -> 2.34 us
    ppermute x15, waiting for transfers between devices: 26.9 us -> 24.2 us  [local(): lax.ppermute(x, 'row', [(r, r ^ bit) for r in range(rows_n)])]
  transfers between devices with their start and end apart: 27 -> 27, of which waited for: 12 -> 15; matrix products, arithmetic and copies ran while one was open for 12% -> 12% of each run, Pallas kernels for 30% -> 30%
where the time goes in v1:
time: 159 us; the launch traced here: 158 us
  Pallas kernels  55.7 us (35%)
  waiting for transfers between devices  54.7 us (34%)
  starting transfers between devices  25.3 us (16%)
  matrix products  13.9 us (9%)
  other arithmetic  4.79 us (3%)
  local copies, waits for them, and re-layouts  3.18 us (2%)
    pallas_call x3, Pallas kernels, chunk_dot(): pl.pallas_call(kernel, grid_spec=pltpu.PrefetchScalarGridSpec(num_scalar_...  39.6 us
    ppermute x15, waiting for transfers between devices, local(): lax.ppermute(x, 'row', [(r, r ^ bit) for r in range(rows_n)])  24.2 us
    ppermute x3, waiting for transfers between devices, local(): block = lax.ppermute(blocks[-1], 'col', ring)  18 us
    pallas_call x2, Pallas kernels, lambda_product(): pl.pallas_call(kernel, grid_spec=pltpu.PrefetchScalarGridSpec(num_scalar_...  16.1 us
    ppermute x15, starting transfers between devices, local(): lax.ppermute(x, 'row', [(r, r ^ bit) for r in range(rows_n)])  16 us
    dot_general x1, matrix products, first_chunk_dot(): jnp.dot(gate(jnp.concatenate(blocks, axis=0), *after), basis[:, start:sta...  11.5 us
    ppermute x3, waiting for transfers between devices, local(): lax.ppermute(x, 'col', on_both_cores([(c, c ^ bit) for c in range(chips)]))  11 us
    ppermute x3, starting transfers between devices, local(): block = lax.ppermute(blocks[-1], 'col', ring)  4.36 us
  transfers between devices with their start and end apart: 27, of which 15 were waited for; matrix products, arithmetic and copies ran while one was open for 12% of the time, Pallas kernels for 30%

profile of v1, /device:TPU:0, one launch (start us, length us, event | category | flops | bytes accessed | tf_op | source)
XLA Modules:
  0.0 157.9 jit_solution(1812964536259344339)
XLA Ops:
  0.5 2.6 %collective-permute-start = (bf16[64,7168]{1,0:T(8,128)(2,1)}, bf16[64,7168]{1,0:T(8,128)(2,1)S(1)}, u32[]{:S(2)}, u32[]{:S(2)}) collective-permute-start(bf16[64,7168]{1,0:T(8,128)(2,1)} %rest_0_.1), channel_id=1, source_target_pairs={{0,2},{1,3},{2,6},{3,7},{4,0},{5,1},{6,4},{7,5},{8,10},{9,11},{10,... | collective-permute-start | bytes 2752520 | tf_op jit(solution)/shard_map/ppermute | solution.py:235
  4.0 2.7 %collective-permute-start.4 = (bf16[128,1024]{1,0:T(8,128)(2,1)S(1)}, bf16[128,1024]{1,0:T(8,128)(2,1)S(1)}, u32[]{:S(2)}, u32[]{:S(2)}) collective-permute-start(bf16[128,1024]{1,0:T(8,128)(2,1)S(1)} %copy_gate.1), channel_id=1, source_target_pairs={{0,8},{8,0},{16,24},{24,16},{1,9},{9,1},{17,25},{25,17},{2,10},{10... | collective-permute-start | bytes 786440 | tf_op jit(solution)/shard_map/ppermute | solution.py:218
  9.0 4.7 %collective-permute-done.4 = bf16[128,1024]{1,0:T(8,128)(2,1)S(1)} collective-permute-done((bf16[128,1024]{1,0:T(8,128)(2,1)S(1)}, bf16[128,1024]{1,0:T(8,128)(2,1)S(1)}, u32[]{:S(2)}, u32[]{:S(2)}) %collective-permute-start.4) | collective-permute-done | bytes 262176 | tf_op jit(solution)/shard_map/ppermute | solution.py:218
  13.9 6.5 %collective-permute-done.3 = bf16[128,1024]{1,0:T(8,128)(2,1)S(1)} collective-permute-done((bf16[128,1024]{1,0:T(8,128)(2,1)S(1)}, bf16[128,1024]{1,0:T(8,128)(2,1)S(1)}, u32[]{:S(2)}, u32[]{:S(2)}) %collective-permute-start.3) | collective-permute-done | bytes 262176 | tf_op jit(solution)/shard_map/ppermute | solution.py:218
  21.0 4.3 %collective-permute-done.refs_0_ = bf16[64,7168]{1,0:T(8,128)(2,1)S(1)} collective-permute-done((bf16[64,7168]{1,0:T(8,128)(2,1)}, bf16[64,7168]{1,0:T(8,128)(2,1)S(1)}, u32[]{:S(2)}, u32[]{:S(2)}) %collective-permute-start) | collective-permute-done | bytes 917536 | tf_op jit(solution)/shard_map/ppermute | solution.py:235
  26.2 2.4 %convolution_bitcast_fusion = f32[2048,512]{1,0:T(8,128)S(1)} fusion(bf16[512,1024]{1,0:T(8,128)(2,1)S(1)} %maximum_select_fusion.refs_1_, bf16[1024,2048]{1,0:T(8,128)(2,1)S(1)} %copy-done.4), kind=kOutput, calls=%fused_computation.3 | convolution fusion | flops 2147483648 | bytes 9437184 | tf_op jit(solution)/shard_map/dot_general | solution.py:260
  30.8 11.5 %fusion.2 = bf16[256,1792]{1,0:T(8,128)(2,1)S(1)} fusion(bf16[256,7168]{1,0:T(8,128)(2,1)S(1)} %gates.10, bf16[7168,3584]{1,0:T(8,128)(2,1)} %rest_4_.5), kind=kOutput, calls=%fused_computation.4 | convolution fusion | flops 6577127424 | bytes 30277632 | tf_op jit(solution)/shard_map/dot_general | solution.py:126
  42.3 6.6 %collective-permute-done.5.rest_5_.rest_0_ = bf16[64,7168]{1,0:T(8,128)(2,1)S(1)} collective-permute-done((bf16[64,7168]{1,0:T(8,128)(2,1)S(1)}, bf16[64,7168]{1,0:T(8,128)(2,1)S(1)}, u32[]{:S(2)}, u32[]{:S(2)}) %collective-permute-start.5) | collective-permute-done | bytes 917536 | tf_op jit(solution)/shard_map/ppermute | solution.py:235
  51.4 13.3 %chunk_dot.3 = (bf16[128,1792]{1,0:T(8,128)(2,1)S(1)}, bf16[128,1792]{1,0:T(8,128)(2,1)S(1)}) custom-call(s32[1]{0:T(128)} %bitcast.2.upper_ref, bf16[64,7168]{1,0:T(8,128)(2,1)S(1)} %copy-done, bf16[64,7168]{1,0:T(8,128)(2,1)S(1)} %collective-permute-done.1.after_ref.rest_1_, bf16[64,7168]{1,0:T(8,128)(2,1)S(1)} %gates.9.rest_2_, ...), custom_call_target="tpu_custom_call" | custom-call | flops 6576668672 | bytes 25690112 | tf_op jit(solution)/shard_map/chunk_dot/pallas_call | solution.py:103
  64.7 7.1 %collective-permute-done.7.rest_2_ = bf16[64,7168]{1,0:T(8,128)(2,1)S(1)} collective-permute-done((bf16[64,7168]{1,0:T(8,128)(2,1)S(1)}, bf16[64,7168]{1,0:T(8,128)(2,1)S(1)}, u32[]{:S(2)}, u32[]{:S(2)}) %collective-permute-start.7) | collective-permute-done | bytes 917536 | tf_op jit(solution)/shard_map/ppermute | solution.py:235
  71.8 1.6 %convert_add_fusion = f32[2048,256]{1,0:T(8,128)S(1)} fusion(bf16[2048,256]{1,0:T(8,128)(2,1)} %collective-permute-done.11, f32[2048,512]{1,0:T(8,128)S(1)} %copy-done.3, pred[]{:T(512)S(6)} %eq.4), kind=kLoop, calls=%fused_computation.5 | loop fusion | flops 1572864 | bytes 7340033 | tf_op jit(solution)/shard_map/add | solution.py:270
  73.8 1.6 %collective-permute-start.12 = (bf16[128,1792]{1,0:T(8,128)(2,1)S(1)}, bf16[128,1792]{1,0:T(8,128)(2,1)S(1)}, u32[]{:S(2)}, u32[]{:S(2)}) collective-permute-start(bf16[128,1792]{1,0:T(8,128)(2,1)S(1)} %get-tuple-element.32.rest_5_), channel_id=1, source_target_pairs={{0,16},{8,24},{16,0},{24,8},{1,17},{9,25},{17,1},{25,9},{2,18},{10... | collective-permute-start | bytes 1376264 | tf_op jit(solution)/shard_map/ppermute | solution.py:218
  77.7 13.1 %chunk_dot.4 = (bf16[128,1792]{1,0:T(8,128)(2,1)S(1)}, bf16[128,1792]{1,0:T(8,128)(2,1)S(1)}) custom-call(s32[1]{0:T(128)} %bitcast.1.upper_ref, bf16[64,7168]{1,0:T(8,128)(2,1)S(1)} %collective-permute-done.5.rest_5_.rest_0_, bf16[64,7168]{1,0:T(8,128)(2,1)S(1)} %collective-permute-done.6.rest_1_, bf16[64,7168]{1,0:T(8,128)(2,1)S(1)} %collective-permute-done.7.rest_2_, ...), custom_call_target="tpu_custom_call" | custom-call | flops 6576668672 | bytes 25690112 | tf_op jit(solution)/shard_map/chunk_dot/pallas_call | solution.py:103
  93.9 3.4 %collective-permute-start.21 = (bf16[1024,256]{1,0:T(8,128)(2,1)S(1)}, bf16[1024,256]{1,0:T(8,128)(2,1)S(1)}, u32[]{:S(2)}, u32[]{:S(2)}) collective-permute-start(bf16[1024,256]{1,0:T(8,128)(2,1)S(1)} %get-tuple-element.52), channel_id=1, source_target_pairs={{0,4},{1,5},{2,6},{3,7},{4,0},{5,1},{6,2},{7,3},{8,12},{9,13},{10,... | collective-permute-start | bytes 1572872 | tf_op jit(solution)/shard_map/ppermute | solution.py:242
  97.3 13.2 %chunk_dot.5 = (bf16[128,1792]{1,0:T(8,128)(2,1)S(1)}, bf16[128,1792]{1,0:T(8,128)(2,1)S(1)}) custom-call(s32[1]{0:T(128)} %bitcast.1.upper_ref, bf16[64,7168]{1,0:T(8,128)(2,1)S(1)} %collective-permute-done.5.rest_5_.rest_0_, bf16[64,7168]{1,0:T(8,128)(2,1)S(1)} %collective-permute-done.6.rest_1_, bf16[64,7168]{1,0:T(8,128)(2,1)S(1)} %collective-permute-done.7.rest_2_, ...), custom_call_target="tpu_custom_call" | custom-call | flops 6576668672 | bytes 25690112 | tf_op jit(solution)/shard_map/chunk_dot/pallas_call | solution.py:103
  110.6 2.7 %collective-permute-done.15.refs_0_ = bf16[128,1792]{1,0:T(8,128)(2,1)S(1)} collective-permute-done((bf16[128,1792]{1,0:T(8,128)(2,1)S(1)}, bf16[128,1792]{1,0:T(8,128)(2,1)S(1)}, u32[]{:S(2)}, u32[]{:S(2)}) %collective-permute-start.15) | collective-permute-done | bytes 458784 | tf_op jit(solution)/shard_map/ppermute | solution.py:218
  114.7 4.7 %collective-permute-done.21 = bf16[1024,256]{1,0:T(8,128)(2,1)S(1)} collective-permute-done((bf16[1024,256]{1,0:T(8,128)(2,1)S(1)}, bf16[1024,256]{1,0:T(8,128)(2,1)S(1)}, u32[]{:S(2)}, u32[]{:S(2)}) %collective-permute-start.21) | collective-permute-done | bytes 524320 | tf_op jit(solution)/shard_map/ppermute | solution.py:242
  119.8 5.0 %collective-permute-done.18 = bf16[128,1792]{1,0:T(8,128)(2,1)S(1)} collective-permute-done((bf16[128,1792]{1,0:T(8,128)(2,1)S(1)}, bf16[128,1792]{1,0:T(8,128)(2,1)S(1)}, u32[]{:S(2)}, u32[]{:S(2)}) %collective-permute-start.18) | collective-permute-done | bytes 458784 | tf_op jit(solution)/shard_map/ppermute | solution.py:218
  125.2 1.6 %collective-permute-start.20 = (bf16[128,1792]{1,0:T(8,128)(2,1)S(1)}, bf16[128,1792]{1,0:T(8,128)(2,1)S(1)}, u32[]{:S(2)}, u32[]{:S(2)}) collective-permute-start(bf16[128,1792]{1,0:T(8,128)(2,1)S(1)} %get-tuple-element.50), channel_id=1, source_target_pairs={{0,16},{8,24},{16,0},{24,8},{1,17},{9,25},{17,1},{25,9},{2,18},{10... | collective-permute-start | bytes 1376264 | tf_op jit(solution)/shard_map/ppermute | solution.py:218
  127.3 6.3 %collective-permute-done.22 = bf16[1024,256]{1,0:T(8,128)(2,1)S(1)} collective-permute-done((bf16[1024,256]{1,0:T(8,128)(2,1)S(1)}, bf16[1024,256]{1,0:T(8,128)(2,1)S(1)}, u32[]{:S(2)}, u32[]{:S(2)}) %collective-permute-start.22) | collective-permute-done | bytes 524320 | tf_op jit(solution)/shard_map/ppermute | solution.py:242
  133.9 1.6 %collective-permute-done.20 = bf16[128,1792]{1,0:T(8,128)(2,1)S(1)} collective-permute-done((bf16[128,1792]{1,0:T(8,128)(2,1)S(1)}, bf16[128,1792]{1,0:T(8,128)(2,1)S(1)}, u32[]{:S(2)}, u32[]{:S(2)}) %collective-permute-start.20) | collective-permute-done | bytes 458784 | tf_op jit(solution)/shard_map/ppermute | solution.py:218
  139.1 8.1 %lambda_product.2.rest_4_ = bf16[2048,3584]{1,0:T(8,128)(2,1)} custom-call(s32[8]{0:T(128)S(1)} %dynamic-slice_bitcast_fusion.refs_2_.place_ref, bf16[2048,256]{1,0:T(8,128)(2,1)S(1)} %get-tuple-element.54.own_ref, bf16[2048,256]{1,0:T(8,128)(2,1)S(1)} %collective-permute-done.24.sib_ref, bf16[128,1792]{1,0:T(8,128)(2,1)S(1)} %get-tuple-element.44.rest_0_, ...), custom_call_target="tpu_custom_call" | custom-call | flops 3758096384 | bytes 7340032 | tf_op jit(solution)/shard_map/lambda_product/pallas_call | solution.py:161
  147.2 2.2 %collective-permute-done.25.rest_1_ = bf16[128,1792]{1,0:T(8,128)(2,1)S(1)} collective-permute-done((bf16[128,1792]{1,0:T(8,128)(2,1)S(1)}, bf16[128,1792]{1,0:T(8,128)(2,1)S(1)}, u32[]{:S(2)}, u32[]{:S(2)}) %collective-permute-start.25) | collective-permute-done | bytes 458784 | tf_op jit(solution)/shard_map/ppermute | solution.py:218
  149.9 8.1 %lambda_product.3 = bf16[2048,3584]{1,0:T(8,128)(2,1)} custom-call(s32[8]{0:T(128)S(1)} %dynamic-slice_bitcast_fusion.refs_2_.place_ref, bf16[2048,256]{1,0:T(8,128)(2,1)S(1)} %get-tuple-element.54.own_ref, bf16[2048,256]{1,0:T(8,128)(2,1)S(1)} %collective-permute-done.24.sib_ref, ...), custom_call_target="tpu_custom_call", output_to_operand_aliasing={{}: (7, {})} | custom-call | flops 3758096384 | bytes 7340032 | tf_op jit(solution)/shard_map/lambda_product/pallas_call | solution.py:161
  (76 shorter events, 22.7 us)
Async XLA Ops:
  0.5 24.8 %collective-permute-start = (bf16[64,7168]{1,0:T(8,128)(2,1)}, bf16[64,7168]{1,0:T(8,128)(2,1)S(1)}, u32[]{:S(2)}, u32[]{:S(2)}) collective-permute-start(bf16[64,7168]{1,0:T(8,128)(2,1)} %rest_0_.1), channel_id=1, source_target_pairs={{0,2},{1,3},{2,6},{3,7},{4,0},{5,1},{6,4},{7,5},{8,10},{9,11},{10,... | collective-permute-start | bytes 2752520 | tf_op jit(solution)/shard_map/ppermute | solution.py:235
  4.0 9.7 %collective-permute-start.4 = (bf16[128,1024]{1,0:T(8,128)(2,1)S(1)}, bf16[128,1024]{1,0:T(8,128)(2,1)S(1)}, u32[]{:S(2)}, u32[]{:S(2)}) collective-permute-start(bf16[128,1024]{1,0:T(8,128)(2,1)S(1)} %copy_gate.1), channel_id=1, source_target_pairs={{0,8},{8,0},{16,24},{24,16},{1,9},{9,1},{17,25},{25,17},{2,10},{10... | collective-permute-start | bytes 786440 | tf_op jit(solution)/shard_map/ppermute | solution.py:218
  6.7 13.7 %collective-permute-start.3 = (bf16[128,1024]{1,0:T(8,128)(2,1)S(1)}, bf16[128,1024]{1,0:T(8,128)(2,1)S(1)}, u32[]{:S(2)}, u32[]{:S(2)}) collective-permute-start(bf16[128,1024]{1,0:T(8,128)(2,1)S(1)} %copy_gate.1), channel_id=1, source_target_pairs={{0,16},{8,24},{16,0},{24,8},{1,17},{9,25},{17,1},{25,9},{2,18},{10... | collective-permute-start | bytes 786440 | tf_op jit(solution)/shard_map/ppermute | solution.py:218
  8.2 12.2 %collective-permute-start.2 = (bf16[128,1024]{1,0:T(8,128)(2,1)S(1)}, bf16[128,1024]{1,0:T(8,128)(2,1)S(1)}, u32[]{:S(2)}, u32[]{:S(2)}) collective-permute-start(bf16[128,1024]{1,0:T(8,128)(2,1)S(1)} %copy_gate.1), channel_id=1, source_target_pairs={{0,24},{8,16},{16,8},{24,0},{1,25},{9,17},{17,9},{25,1},{2,26},{10... | collective-permute-start | bytes 786440 | tf_op jit(solution)/shard_map/ppermute | solution.py:218
  25.3 23.7 %collective-permute-start.5 = (bf16[64,7168]{1,0:T(8,128)(2,1)S(1)}, bf16[64,7168]{1,0:T(8,128)(2,1)S(1)}, u32[]{:S(2)}, u32[]{:S(2)}) collective-permute-start(bf16[64,7168]{1,0:T(8,128)(2,1)S(1)} %gates.9.rest_2_), channel_id=1, source_target_pairs={{0,2},{1,3},{2,6},{3,7},{4,0},{5,1},{6,4},{7,5},{8,10},{9,11},{10,... | collective-permute-start | bytes 2752520 | tf_op jit(solution)/shard_map/ppermute | solution.py:235
  28.8 43.0 %collective-permute-start.11 = (bf16[2048,256]{1,0:T(8,128)(2,1)S(1)}, bf16[2048,256]{1,0:T(8,128)(2,1)}, u32[]{:S(2)}, u32[]{:S(2)}) collective-permute-start(bf16[2048,256]{1,0:T(8,128)(2,1)S(1)} %select_convert_fusion.refs_1_), channel_id=1, source_target_pairs={{0,1},{1,0},{2,3},{3,2},{4,5},{5,4},{6,7},{7,6},{8,9},{9,8},{10,11... | collective-permute-start | bytes 3145736 | tf_op jit(solution)/shard_map/ppermute | solution.py:217
  48.9 22.9 %collective-permute-start.7 = (bf16[64,7168]{1,0:T(8,128)(2,1)S(1)}, bf16[64,7168]{1,0:T(8,128)(2,1)S(1)}, u32[]{:S(2)}, u32[]{:S(2)}) collective-permute-start(bf16[64,7168]{1,0:T(8,128)(2,1)S(1)} %collective-permute-done.5.rest_5_.rest_0_), channel_id=1, source_target_pairs={{0,2},{1,3},{2,6},{3,7},{4,0},{5,1},{6,4},{7,5},{8,10},{9,11},{10,... | collective-permute-start | bytes 2752520 | tf_op jit(solution)/shard_map/ppermute | solution.py:235
  49.8 23.7 %collective-permute-start.10 = (bf16[128,1792]{1,0:T(8,128)(2,1)S(1)}, bf16[128,1792]{1,0:T(8,128)(2,1)S(1)}, u32[]{:S(2)}, u32[]{:S(2)}) collective-permute-start(bf16[128,1792]{1,0:T(8,128)(2,1)S(1)} %broadcast_select_fusion.rest_6_), channel_id=1, source_target_pairs={{0,16},{8,24},{16,0},{24,8},{1,17},{9,25},{17,1},{25,9},{2,18},{10... | collective-permute-start | bytes 1376264 | tf_op jit(solution)/shard_map/ppermute | solution.py:218
  51.4 26.3 %collective-permute-start.6 = (bf16[64,7168]{1,0:T(8,128)(2,1)S(1)}, bf16[64,7168]{1,0:T(8,128)(2,1)S(1)}, u32[]{:S(2)}, u32[]{:S(2)}) collective-permute-start(bf16[64,7168]{1,0:T(8,128)(2,1)S(1)} %collective-permute-done.5.rest_5_.rest_0_), channel_id=1, source_target_pairs={{0,1},{1,0},{2,3},{3,2},{4,5},{5,4},{6,7},{7,6},{8,9},{9,8},{10,11... | collective-permute-start | bytes 2752520 | tf_op jit(solution)/shard_map/ppermute | solution.py:217
  71.8 5.9 %collective-permute-start.8 = (bf16[64,7168]{1,0:T(8,128)(2,1)S(1)}, bf16[64,7168]{1,0:T(8,128)(2,1)S(1)}, u32[]{:S(2)}, u32[]{:S(2)}) collective-permute-start(bf16[64,7168]{1,0:T(8,128)(2,1)S(1)} %collective-permute-done.7.rest_2_), channel_id=1, source_target_pairs={{0,1},{1,0},{2,3},{3,2},{4,5},{5,4},{6,7},{7,6},{8,9},{9,8},{10,11... | collective-permute-start | bytes 2752520 | tf_op jit(solution)/shard_map/ppermute | solution.py:217
  73.8 17.0 %collective-permute-start.12 = (bf16[128,1792]{1,0:T(8,128)(2,1)S(1)}, bf16[128,1792]{1,0:T(8,128)(2,1)S(1)}, u32[]{:S(2)}, u32[]{:S(2)}) collective-permute-start(bf16[128,1792]{1,0:T(8,128)(2,1)S(1)} %get-tuple-element.32.rest_5_), channel_id=1, source_target_pairs={{0,16},{8,24},{16,0},{24,8},{1,17},{9,25},{17,1},{25,9},{2,18},{10... | collective-permute-start | bytes 1376264 | tf_op jit(solution)/shard_map/ppermute | solution.py:218
  75.4 15.4 %collective-permute-start.13 = (bf16[128,1792]{1,0:T(8,128)(2,1)S(1)}, bf16[128,1792]{1,0:T(8,128)(2,1)S(1)}, u32[]{:S(2)}, u32[]{:S(2)}) collective-permute-start(bf16[128,1792]{1,0:T(8,128)(2,1)S(1)} %get-tuple-element.34), channel_id=1, source_target_pairs={{0,8},{8,0},{16,24},{24,16},{1,9},{9,1},{17,25},{25,17},{2,10},{10... | collective-permute-start | bytes 1376264 | tf_op jit(solution)/shard_map/ppermute | solution.py:218
  76.9 13.9 %collective-permute-start.14 = (bf16[1024,256]{1,0:T(8,128)(2,1)S(1)}, bf16[1024,256]{1,0:T(8,128)(2,1)S(1)}, u32[]{:S(2)}, u32[]{:S(2)}) collective-permute-start(bf16[1024,256]{1,0:T(8,128)(2,1)S(1)} %get-tuple-element.35), channel_id=1, source_target_pairs={{0,2},{1,3},{2,0},{3,1},{4,6},{5,7},{6,4},{7,5},{8,10},{9,11},{10,... | collective-permute-start | bytes 1572872 | tf_op jit(solution)/shard_map/ppermute | solution.py:242
  91.3 19.2 %collective-permute-start.16 = (bf16[128,1792]{1,0:T(8,128)(2,1)S(1)}, bf16[128,1792]{1,0:T(8,128)(2,1)S(1)}, u32[]{:S(2)}, u32[]{:S(2)}) collective-permute-start(bf16[128,1792]{1,0:T(8,128)(2,1)S(1)} %get-tuple-element.40.rest_5_), channel_id=1, source_target_pairs={{0,8},{8,0},{16,24},{24,16},{1,9},{9,1},{17,25},{25,17},{2,10},{10... | collective-permute-start | bytes 1376264 | tf_op jit(solution)/shard_map/ppermute | solution.py:218
  91.9 21.4 %collective-permute-start.15 = (bf16[128,1792]{1,0:T(8,128)(2,1)S(1)}, bf16[128,1792]{1,0:T(8,128)(2,1)S(1)}, u32[]{:S(2)}, u32[]{:S(2)}) collective-permute-start(bf16[128,1792]{1,0:T(8,128)(2,1)S(1)} %get-tuple-element.43), channel_id=1, source_target_pairs={{0,8},{8,0},{16,24},{24,16},{1,9},{9,1},{17,25},{25,17},{2,10},{10... | collective-permute-start | bytes 1376264 | tf_op jit(solution)/shard_map/ppermute | solution.py:218
  93.4 19.9 %collective-permute-start.17 = (bf16[128,1792]{1,0:T(8,128)(2,1)S(1)}, bf16[128,1792]{1,0:T(8,128)(2,1)S(1)}, u32[]{:S(2)}, u32[]{:S(2)}) collective-permute-start(bf16[128,1792]{1,0:T(8,128)(2,1)S(1)} %get-tuple-element.44.rest_0_), channel_id=1, source_target_pairs={{0,16},{8,24},{16,0},{24,8},{1,17},{9,25},{17,1},{25,9},{2,18},{10... | collective-permute-start | bytes 1376264 | tf_op jit(solution)/shard_map/ppermute | solution.py:218
  93.9 25.5 %collective-permute-start.21 = (bf16[1024,256]{1,0:T(8,128)(2,1)S(1)}, bf16[1024,256]{1,0:T(8,128)(2,1)S(1)}, u32[]{:S(2)}, u32[]{:S(2)}) collective-permute-start(bf16[1024,256]{1,0:T(8,128)(2,1)S(1)} %get-tuple-element.52), channel_id=1, source_target_pairs={{0,4},{1,5},{2,6},{3,7},{4,0},{5,1},{6,2},{7,3},{8,12},{9,13},{10,... | collective-permute-start | bytes 1572872 | tf_op jit(solution)/shard_map/ppermute | solution.py:242
  113.6 11.3 %collective-permute-start.18 = (bf16[128,1792]{1,0:T(8,128)(2,1)S(1)}, bf16[128,1792]{1,0:T(8,128)(2,1)S(1)}, u32[]{:S(2)}, u32[]{:S(2)}) collective-permute-start(bf16[128,1792]{1,0:T(8,128)(2,1)S(1)} %get-tuple-element.47), channel_id=1, source_target_pairs={{0,16},{8,24},{16,0},{24,8},{1,17},{9,25},{17,1},{25,9},{2,18},{10... | collective-permute-start | bytes 1376264 | tf_op jit(solution)/shard_map/ppermute | solution.py:218
  114.1 10.9 %collective-permute-start.19 = (bf16[128,1792]{1,0:T(8,128)(2,1)S(1)}, bf16[128,1792]{1,0:T(8,128)(2,1)S(1)}, u32[]{:S(2)}, u32[]{:S(2)}) collective-permute-start(bf16[128,1792]{1,0:T(8,128)(2,1)S(1)} %get-tuple-element.49), channel_id=1, source_target_pairs={{0,8},{8,0},{16,24},{24,16},{1,9},{9,1},{17,25},{25,17},{2,10},{10... | collective-permute-start | bytes 1376264 | tf_op jit(solution)/shard_map/ppermute | solution.py:218
  119.7 13.9 %collective-permute-start.22 = (bf16[1024,256]{1,0:T(8,128)(2,1)S(1)}, bf16[1024,256]{1,0:T(8,128)(2,1)S(1)}, u32[]{:S(2)}, u32[]{:S(2)}) collective-permute-start(bf16[1024,256]{1,0:T(8,128)(2,1)S(1)} %add_convert_fusion), channel_id=1, source_target_pairs={{0,2},{1,3},{2,0},{3,1},{4,6},{5,7},{6,4},{7,5},{8,10},{9,11},{10,... | collective-permute-start | bytes 1572872 | tf_op jit(solution)/shard_map/ppermute | solution.py:242
  125.2 10.3 %collective-permute-start.20 = (bf16[128,1792]{1,0:T(8,128)(2,1)S(1)}, bf16[128,1792]{1,0:T(8,128)(2,1)S(1)}, u32[]{:S(2)}, u32[]{:S(2)}) collective-permute-start(bf16[128,1792]{1,0:T(8,128)(2,1)S(1)} %get-tuple-element.50), channel_id=1, source_target_pairs={{0,16},{8,24},{16,0},{24,8},{1,17},{9,25},{17,1},{25,9},{2,18},{10... | collective-permute-start | bytes 1376264 | tf_op jit(solution)/shard_map/ppermute | solution.py:218
  126.8 9.7 %collective-permute-start.23 = (bf16[128,1792]{1,0:T(8,128)(2,1)S(1)}, bf16[128,1792]{1,0:T(8,128)(2,1)S(1)}, u32[]{:S(2)}, u32[]{:S(2)}) collective-permute-start(bf16[128,1792]{1,0:T(8,128)(2,1)S(1)} %get-tuple-element.53.rest_2_), channel_id=1, source_target_pairs={{0,8},{8,0},{16,24},{24,16},{1,9},{9,1},{17,25},{25,17},{2,10},{10... | collective-permute-start | bytes 1376264 | tf_op jit(solution)/shard_map/ppermute | solution.py:218
  136.5 12.9 %collective-permute-start.25 = (bf16[128,1792]{1,0:T(8,128)(2,1)S(1)}, bf16[128,1792]{1,0:T(8,128)(2,1)S(1)}, u32[]{:S(2)}, u32[]{:S(2)}) collective-permute-start(bf16[128,1792]{1,0:T(8,128)(2,1)S(1)} %get-tuple-element.55.rest_0_), channel_id=1, source_target_pairs={{0,16},{8,24},{16,0},{24,8},{1,17},{9,25},{17,1},{25,9},{2,18},{10... | collective-permute-start | bytes 1376264 | tf_op jit(solution)/shard_map/ppermute | solution.py:218
  137.2 12.7 %collective-permute-start.26 = (bf16[128,1792]{1,0:T(8,128)(2,1)S(1)}, bf16[128,1792]{1,0:T(8,128)(2,1)S(1)}, u32[]{:S(2)}, u32[]{:S(2)}) collective-permute-start(bf16[128,1792]{1,0:T(8,128)(2,1)S(1)} %get-tuple-element.56.rest_2_), channel_id=1, source_target_pairs={{0,8},{8,0},{16,24},{24,16},{1,9},{9,1},{17,25},{25,17},{2,10},{10... | collective-permute-start | bytes 1376264 | tf_op jit(solution)/shard_map/ppermute | solution.py:218
  (8 other events, 52.9 us)

commit v2 on v1

--- a/solution.py
+++ b/solution.py
@@ -134,7 +134,7 @@
 def lambda_product(place, own, sib, parts, unit, start, width, whole, so_far=None):
     out_rows, seq_tokens = own.shape
     tile_o = largest_tile(out_rows, 128, 256)
-    tile_n = width // 2 if width % 256 == 0 else width
+    tile_n = min(512, width)
     at_block = start // width
     count = len(parts)
     given = [] if so_far is None else [so_far]
@@ -303,6 +303,8 @@
     got_r = trade(send_r, early_bit)
     got_l = trade(keep_l, early_bits[0])
     got_away = chip_trade(away, 1)
+    last = gate(blocks[-1], send_r)
+    late[-2:] = [last, swap(last)]
     late_l, send_l = chunk_dot(late, act_basis, start_l, wide_l, [send_r], late_upper)
 
     got_r, got_l, got_away = gates([got_r, got_l, got_away], send_l)

time: 159 us -> 157 us (0.987)
  waiting for transfers between devices: 54.7 us -> 50.5 us
  starting transfers between devices: 25.3 us -> 28.5 us
    ppermute x15, starting transfers between devices: 16 us -> 18.9 us  [local(): lax.ppermute(x, 'row', [(r, r ^ bit) for r in range(rows_n)])]
    ppermute x3, waiting for transfers between devices: 18 us -> 16 us  [local(): block = lax.ppermute(blocks[-1], 'col', ring)]
    ppermute x3, waiting for transfers between devices: 11 us -> 9.07 us  [local(): lax.ppermute(x, 'col', on_both_cores([(c, c ^ bit) for c in range(chips)]))]
  transfers between devices with their start and end apart: 27 -> 27, of which waited for: 15 -> 14; matrix products, arithmetic and copies ran while one was open for 12% -> 12% of each run, Pallas kernels for 30% -> 30%
where the time goes in v2:
time: 157 us; the launch traced here: 156 us
  Pallas kernels  55.1 us (35%)
  waiting for transfers between devices  50.5 us (32%)
  starting transfers between devices  28.5 us (18%)
  matrix products  13.9 us (9%)
  other arithmetic  4.69 us (3%)
  local copies, waits for them, and re-layouts  3.19 us (2%)
    pallas_call x3, Pallas kernels, chunk_dot(): pl.pallas_call(kernel, grid_spec=pltpu.PrefetchScalarGridSpec(num_scalar_...  39.6 us
    ppermute x15, waiting for transfers between devices, local(): lax.ppermute(x, 'row', [(r, r ^ bit) for r in range(rows_n)])  25.5 us
    ppermute x15, starting transfers between devices, local(): lax.ppermute(x, 'row', [(r, r ^ bit) for r in range(rows_n)])  18.9 us
    ppermute x3, waiting for transfers between devices, local(): block = lax.ppermute(blocks[-1], 'col', ring)  16 us
    pallas_call x2, Pallas kernels, lambda_product(): pl.pallas_call(kernel, grid_spec=pltpu.PrefetchScalarGridSpec(num_scalar_...  15.4 us
    dot_general x1, matrix products, first_chunk_dot(): jnp.dot(gate(jnp.concatenate(blocks, axis=0), *after), basis[:, start:sta...  11.5 us
    ppermute x3, waiting for transfers between devices, local(): lax.ppermute(x, 'col', on_both_cores([(c, c ^ bit) for c in range(chips)]))  9.07 us
    ppermute x3, starting transfers between devices, local(): lax.ppermute(x, 'col', on_both_cores([(c, c ^ bit) for c in range(chips)]))  4.42 us
  transfers between devices with their start and end apart: 27, of which 14 were waited for; matrix products, arithmetic and copies ran while one was open for 12% of the time, Pallas kernels for 30%

profile of v2, /device:TPU:0, one launch (start us, length us, event | category | flops | bytes accessed | tf_op | source)
XLA Modules:
  0.0 156.2 jit_solution(9816273490048409361)
XLA Ops:
  0.5 2.6 %collective-permute-start = (bf16[64,7168]{1,0:T(8,128)(2,1)}, bf16[64,7168]{1,0:T(8,128)(2,1)S(1)}, u32[]{:S(2)}, u32[]{:S(2)}) collective-permute-start(bf16[64,7168]{1,0:T(8,128)(2,1)} %rest_0_.1), channel_id=1, source_target_pairs={{0,2},{1,3},{2,6},{3,7},{4,0},{5,1},{6,4},{7,5},{8,10},{9,11},{10,... | collective-permute-start | bytes 2752520 | tf_op jit(solution)/shard_map/ppermute | solution.py:235
  4.0 2.7 %collective-permute-start.4 = (bf16[128,1024]{1,0:T(8,128)(2,1)S(1)}, bf16[128,1024]{1,0:T(8,128)(2,1)S(1)}, u32[]{:S(2)}, u32[]{:S(2)}) collective-permute-start(bf16[128,1024]{1,0:T(8,128)(2,1)S(1)} %copy_gate.1), channel_id=1, source_target_pairs={{0,8},{8,0},{16,24},{24,16},{1,9},{9,1},{17,25},{25,17},{2,10},{10... | collective-permute-start | bytes 786440 | tf_op jit(solution)/shard_map/ppermute | solution.py:218
  9.0 4.7 %collective-permute-done.4 = bf16[128,1024]{1,0:T(8,128)(2,1)S(1)} collective-permute-done((bf16[128,1024]{1,0:T(8,128)(2,1)S(1)}, bf16[128,1024]{1,0:T(8,128)(2,1)S(1)}, u32[]{:S(2)}, u32[]{:S(2)}) %collective-permute-start.4) | collective-permute-done | bytes 262176 | tf_op jit(solution)/shard_map/ppermute | solution.py:218
  13.9 6.5 %collective-permute-done.3 = bf16[128,1024]{1,0:T(8,128)(2,1)S(1)} collective-permute-done((bf16[128,1024]{1,0:T(8,128)(2,1)S(1)}, bf16[128,1024]{1,0:T(8,128)(2,1)S(1)}, u32[]{:S(2)}, u32[]{:S(2)}) %collective-permute-start.3) | collective-permute-done | bytes 262176 | tf_op jit(solution)/shard_map/ppermute | solution.py:218
  21.0 4.3 %collective-permute-done.refs_0_ = bf16[64,7168]{1,0:T(8,128)(2,1)S(1)} collective-permute-done((bf16[64,7168]{1,0:T(8,128)(2,1)}, bf16[64,7168]{1,0:T(8,128)(2,1)S(1)}, u32[]{:S(2)}, u32[]{:S(2)}) %collective-permute-start) | collective-permute-done | bytes 917536 | tf_op jit(solution)/shard_map/ppermute | solution.py:235
  26.2 2.4 %convolution_bitcast_fusion = f32[2048,512]{1,0:T(8,128)S(1)} fusion(bf16[512,1024]{1,0:T(8,128)(2,1)S(1)} %maximum_select_fusion.refs_1_, bf16[1024,2048]{1,0:T(8,128)(2,1)S(1)} %copy-done.6), kind=kOutput, calls=%fused_computation.3 | convolution fusion | flops 2147483648 | bytes 9437184 | tf_op jit(solution)/shard_map/dot_general | solution.py:260
  30.8 11.5 %fusion.2 = bf16[256,1792]{1,0:T(8,128)(2,1)S(1)} fusion(bf16[256,7168]{1,0:T(8,128)(2,1)S(1)} %gates.11, bf16[7168,3584]{1,0:T(8,128)(2,1)} %rest_4_.5), kind=kOutput, calls=%fused_computation.4 | convolution fusion | flops 6577127424 | bytes 30277632 | tf_op jit(solution)/shard_map/dot_general | solution.py:126
  42.4 1.6 %collective-permute-start.9 = (bf16[128,1792]{1,0:T(8,128)(2,1)S(1)}, bf16[128,1792]{1,0:T(8,128)(2,1)S(1)}, u32[]{:S(2)}, u32[]{:S(2)}) collective-permute-start(bf16[128,1792]{1,0:T(8,128)(2,1)S(1)} %broadcast_select_fusion.rest_6_), channel_id=1, source_target_pairs={{0,16},{8,24},{16,0},{24,8},{1,17},{9,25},{17,1},{25,9},{2,18},{10... | collective-permute-start | bytes 1376264 | tf_op jit(solution)/shard_map/ppermute | solution.py:218
  44.0 4.9 %collective-permute-done.5.rest_5_.rest_0_ = bf16[64,7168]{1,0:T(8,128)(2,1)S(1)} collective-permute-done((bf16[64,7168]{1,0:T(8,128)(2,1)S(1)}, bf16[64,7168]{1,0:T(8,128)(2,1)S(1)}, u32[]{:S(2)}, u32[]{:S(2)}) %collective-permute-start.5) | collective-permute-done | bytes 917536 | tf_op jit(solution)/shard_map/ppermute | solution.py:235
  49.8 13.3 %chunk_dot.3 = (bf16[128,1792]{1,0:T(8,128)(2,1)S(1)}, bf16[128,1792]{1,0:T(8,128)(2,1)S(1)}) custom-call(s32[1]{0:T(128)} %bitcast.2.upper_ref, bf16[64,7168]{1,0:T(8,128)(2,1)S(1)} %copy-done, bf16[64,7168]{1,0:T(8,128)(2,1)S(1)} %collective-permute-done.1.after_ref.rest_1_, bf16[64,7168]{1,0:T(8,128)(2,1)S(1)} %gates.10.rest_2_, ...), custom_call_target="tpu_custom_call" | custom-call | flops 6576668672 | bytes 25690112 | tf_op jit(solution)/shard_map/chunk_dot/pallas_call | solution.py:103
  63.1 1.7 %convert_add_fusion = f32[2048,256]{1,0:T(8,128)S(1)} fusion(bf16[2048,256]{1,0:T(8,128)(2,1)} %collective-permute-done.10, f32[2048,512]{1,0:T(8,128)S(1)} %copy-done.3, pred[]{:T(512)S(6)} %eq.4), kind=kLoop, calls=%fused_computation.5 | loop fusion | flops 1572864 | bytes 7340033 | tf_op jit(solution)/shard_map/add | solution.py:270
  65.1 6.7 %collective-permute-done.7.refs_0_ = bf16[64,7168]{1,0:T(8,128)(2,1)S(1)} collective-permute-done((bf16[64,7168]{1,0:T(8,128)(2,1)S(1)}, bf16[64,7168]{1,0:T(8,128)(2,1)S(1)}, u32[]{:S(2)}, u32[]{:S(2)}) %collective-permute-start.7) | collective-permute-done | bytes 917536 | tf_op jit(solution)/shard_map/ppermute | solution.py:235
  75.7 13.1 %chunk_dot.4 = (bf16[128,1792]{1,0:T(8,128)(2,1)S(1)}, bf16[128,1792]{1,0:T(8,128)(2,1)S(1)}) custom-call(s32[1]{0:T(128)} %bitcast.1.upper_ref, bf16[64,7168]{1,0:T(8,128)(2,1)S(1)} %collective-permute-done.5.rest_5_.rest_0_, bf16[64,7168]{1,0:T(8,128)(2,1)S(1)} %collective-permute-done.6.rest_1_, bf16[64,7168]{1,0:T(8,128)(2,1)S(1)} %gates.13.rest_2_, ...), custom_call_target="tpu_custom_call" | custom-call | flops 6576668672 | bytes 25690112 | tf_op jit(solution)/shard_map/chunk_dot/pallas_call | solution.py:103
  91.9 3.4 %collective-permute-start.21 = (bf16[1024,256]{1,0:T(8,128)(2,1)S(1)}, bf16[1024,256]{1,0:T(8,128)(2,1)S(1)}, u32[]{:S(2)}, u32[]{:S(2)}) collective-permute-start(bf16[1024,256]{1,0:T(8,128)(2,1)S(1)} %get-tuple-element.52), channel_id=1, source_target_pairs={{0,4},{1,5},{2,6},{3,7},{4,0},{5,1},{6,2},{7,3},{8,12},{9,13},{10,... | collective-permute-start | bytes 1572872 | tf_op jit(solution)/shard_map/ppermute | solution.py:242
  95.2 13.2 %chunk_dot.5 = (bf16[128,1792]{1,0:T(8,128)(2,1)S(1)}, bf16[128,1792]{1,0:T(8,128)(2,1)S(1)}) custom-call(s32[1]{0:T(128)} %bitcast.1.upper_ref, bf16[64,7168]{1,0:T(8,128)(2,1)S(1)} %collective-permute-done.5.rest_5_.rest_0_, bf16[64,7168]{1,0:T(8,128)(2,1)S(1)} %collective-permute-done.6.rest_1_, bf16[64,7168]{1,0:T(8,128)(2,1)S(1)} %gates.13.rest_2_, ...), custom_call_target="tpu_custom_call" | custom-call | flops 6576668672 | bytes 25690112 | tf_op jit(solution)/shard_map/chunk_dot/pallas_call | solution.py:103
  108.5 2.8 %collective-permute-done.15.refs_0_ = bf16[128,1792]{1,0:T(8,128)(2,1)S(1)} collective-permute-done((bf16[128,1792]{1,0:T(8,128)(2,1)S(1)}, bf16[128,1792]{1,0:T(8,128)(2,1)S(1)}, u32[]{:S(2)}, u32[]{:S(2)}) %collective-permute-start.15) | collective-permute-done | bytes 458784 | tf_op jit(solution)/shard_map/ppermute | solution.py:218
  113.7 3.7 %collective-permute-done.21 = bf16[1024,256]{1,0:T(8,128)(2,1)S(1)} collective-permute-done((bf16[1024,256]{1,0:T(8,128)(2,1)S(1)}, bf16[1024,256]{1,0:T(8,128)(2,1)S(1)}, u32[]{:S(2)}, u32[]{:S(2)}) %collective-permute-start.21) | collective-permute-done | bytes 524320 | tf_op jit(solution)/shard_map/ppermute | solution.py:242
  117.9 4.9 %collective-permute-done.18 = bf16[128,1792]{1,0:T(8,128)(2,1)S(1)} collective-permute-done((bf16[128,1792]{1,0:T(8,128)(2,1)S(1)}, bf16[128,1792]{1,0:T(8,128)(2,1)S(1)}, u32[]{:S(2)}, u32[]{:S(2)}) %collective-permute-start.18) | collective-permute-done | bytes 458784 | tf_op jit(solution)/shard_map/ppermute | solution.py:218
  125.7 5.4 %collective-permute-done.22 = bf16[1024,256]{1,0:T(8,128)(2,1)S(1)} collective-permute-done((bf16[1024,256]{1,0:T(8,128)(2,1)S(1)}, bf16[1024,256]{1,0:T(8,128)(2,1)S(1)}, u32[]{:S(2)}, u32[]{:S(2)}) %collective-permute-start.22) | collective-permute-done | bytes 524320 | tf_op jit(solution)/shard_map/ppermute | solution.py:242
  131.4 2.4 %collective-permute-done.20 = bf16[128,1792]{1,0:T(8,128)(2,1)S(1)} collective-permute-done((bf16[128,1792]{1,0:T(8,128)(2,1)S(1)}, bf16[128,1792]{1,0:T(8,128)(2,1)S(1)}, u32[]{:S(2)}, u32[]{:S(2)}) %collective-permute-start.20) | collective-permute-done | bytes 458784 | tf_op jit(solution)/shard_map/ppermute | solution.py:218
  135.8 1.7 %collective-permute-start.26 = (bf16[128,1792]{1,0:T(8,128)(2,1)S(1)}, bf16[128,1792]{1,0:T(8,128)(2,1)S(1)}, u32[]{:S(2)}, u32[]{:S(2)}) collective-permute-start(bf16[128,1792]{1,0:T(8,128)(2,1)S(1)} %get-tuple-element.56.rest_2_), channel_id=1, source_target_pairs={{0,8},{8,0},{16,24},{24,16},{1,9},{9,1},{17,25},{25,17},{2,10},{10... | collective-permute-start | bytes 1376264 | tf_op jit(solution)/shard_map/ppermute | solution.py:218
  137.6 7.7 %lambda_product.2.rest_4_ = bf16[2048,3584]{1,0:T(8,128)(2,1)} custom-call(s32[8]{0:T(128)S(1)} %dynamic-slice_bitcast_fusion.refs_2_.place_ref, bf16[2048,256]{1,0:T(8,128)(2,1)S(1)} %get-tuple-element.54.own_ref, bf16[2048,256]{1,0:T(8,128)(2,1)S(1)} %collective-permute-done.24.sib_ref, bf16[128,1792]{1,0:T(8,128)(2,1)S(1)} %get-tuple-element.44.rest_0_, ...), custom_call_target="tpu_custom_call" | custom-call | flops 3758096384 | bytes 7340032 | tf_op jit(solution)/shard_map/lambda_product/pallas_call | solution.py:161
  145.3 2.1 %collective-permute-done.25.rest_1_ = bf16[128,1792]{1,0:T(8,128)(2,1)S(1)} collective-permute-done((bf16[128,1792]{1,0:T(8,128)(2,1)S(1)}, bf16[128,1792]{1,0:T(8,128)(2,1)S(1)}, u32[]{:S(2)}, u32[]{:S(2)}) %collective-permute-start.25) | collective-permute-done | bytes 458784 | tf_op jit(solution)/shard_map/ppermute | solution.py:218
  148.5 7.7 %lambda_product.3 = bf16[2048,3584]{1,0:T(8,128)(2,1)} custom-call(s32[8]{0:T(128)S(1)} %dynamic-slice_bitcast_fusion.refs_2_.place_ref, bf16[2048,256]{1,0:T(8,128)(2,1)S(1)} %get-tuple-element.54.own_ref, bf16[2048,256]{1,0:T(8,128)(2,1)S(1)} %collective-permute-done.24.sib_ref, ...), custom_call_target="tpu_custom_call", output_to_operand_aliasing={{}: (7, {})} | custom-call | flops 3758096384 | bytes 7340032 | tf_op jit(solution)/shard_map/lambda_product/pallas_call | solution.py:161
  (81 shorter events, 24.9 us)
Async XLA Ops:
  0.5 24.8 %collective-permute-start = (bf16[64,7168]{1,0:T(8,128)(2,1)}, bf16[64,7168]{1,0:T(8,128)(2,1)S(1)}, u32[]{:S(2)}, u32[]{:S(2)}) collective-permute-start(bf16[64,7168]{1,0:T(8,128)(2,1)} %rest_0_.1), channel_id=1, source_target_pairs={{0,2},{1,3},{2,6},{3,7},{4,0},{5,1},{6,4},{7,5},{8,10},{9,11},{10,... | collective-permute-start | bytes 2752520 | tf_op jit(solution)/shard_map/ppermute | solution.py:235
  4.0 9.7 %collective-permute-start.4 = (bf16[128,1024]{1,0:T(8,128)(2,1)S(1)}, bf16[128,1024]{1,0:T(8,128)(2,1)S(1)}, u32[]{:S(2)}, u32[]{:S(2)}) collective-permute-start(bf16[128,1024]{1,0:T(8,128)(2,1)S(1)} %copy_gate.1), channel_id=1, source_target_pairs={{0,8},{8,0},{16,24},{24,16},{1,9},{9,1},{17,25},{25,17},{2,10},{10... | collective-permute-start | bytes 786440 | tf_op jit(solution)/shard_map/ppermute | solution.py:218
  6.7 13.7 %collective-permute-start.3 = (bf16[128,1024]{1,0:T(8,128)(2,1)S(1)}, bf16[128,1024]{1,0:T(8,128)(2,1)S(1)}, u32[]{:S(2)}, u32[]{:S(2)}) collective-permute-start(bf16[128,1024]{1,0:T(8,128)(2,1)S(1)} %copy_gate.1), channel_id=1, source_target_pairs={{0,16},{8,24},{16,0},{24,8},{1,17},{9,25},{17,1},{25,9},{2,18},{10... | collective-permute-start | bytes 786440 | tf_op jit(solution)/shard_map/ppermute | solution.py:218
  8.2 12.2 %collective-permute-start.2 = (bf16[128,1024]{1,0:T(8,128)(2,1)S(1)}, bf16[128,1024]{1,0:T(8,128)(2,1)S(1)}, u32[]{:S(2)}, u32[]{:S(2)}) collective-permute-start(bf16[128,1024]{1,0:T(8,128)(2,1)S(1)} %copy_gate.1), channel_id=1, source_target_pairs={{0,24},{8,16},{16,8},{24,0},{1,25},{9,17},{17,9},{25,1},{2,26},{10... | collective-permute-start | bytes 786440 | tf_op jit(solution)/shard_map/ppermute | solution.py:218
  25.3 23.7 %collective-permute-start.5 = (bf16[64,7168]{1,0:T(8,128)(2,1)S(1)}, bf16[64,7168]{1,0:T(8,128)(2,1)S(1)}, u32[]{:S(2)}, u32[]{:S(2)}) collective-permute-start(bf16[64,7168]{1,0:T(8,128)(2,1)S(1)} %gates.10.rest_2_), channel_id=1, source_target_pairs={{0,2},{1,3},{2,6},{3,7},{4,0},{5,1},{6,4},{7,5},{8,10},{9,11},{10,... | collective-permute-start | bytes 2752520 | tf_op jit(solution)/shard_map/ppermute | solution.py:235
  28.8 34.2 %collective-permute-start.10 = (bf16[2048,256]{1,0:T(8,128)(2,1)S(1)}, bf16[2048,256]{1,0:T(8,128)(2,1)}, u32[]{:S(2)}, u32[]{:S(2)}) collective-permute-start(bf16[2048,256]{1,0:T(8,128)(2,1)S(1)} %select_convert_fusion.refs_1_), channel_id=1, source_target_pairs={{0,1},{1,0},{2,3},{3,2},{4,5},{5,4},{6,7},{7,6},{8,9},{9,8},{10,11... | collective-permute-start | bytes 3145736 | tf_op jit(solution)/shard_map/ppermute | solution.py:217
  42.4 22.5 %collective-permute-start.9 = (bf16[128,1792]{1,0:T(8,128)(2,1)S(1)}, bf16[128,1792]{1,0:T(8,128)(2,1)S(1)}, u32[]{:S(2)}, u32[]{:S(2)}) collective-permute-start(bf16[128,1792]{1,0:T(8,128)(2,1)S(1)} %broadcast_select_fusion.rest_6_), channel_id=1, source_target_pairs={{0,16},{8,24},{16,0},{24,8},{1,17},{9,25},{17,1},{25,9},{2,18},{10... | collective-permute-start | bytes 1376264 | tf_op jit(solution)/shard_map/ppermute | solution.py:218
  48.9 22.9 %collective-permute-start.7 = (bf16[64,7168]{1,0:T(8,128)(2,1)S(1)}, bf16[64,7168]{1,0:T(8,128)(2,1)S(1)}, u32[]{:S(2)}, u32[]{:S(2)}) collective-permute-start(bf16[64,7168]{1,0:T(8,128)(2,1)S(1)} %collective-permute-done.5.rest_5_.rest_0_), channel_id=1, source_target_pairs={{0,2},{1,3},{2,6},{3,7},{4,0},{5,1},{6,4},{7,5},{8,10},{9,11},{10,... | collective-permute-start | bytes 2752520 | tf_op jit(solution)/shard_map/ppermute | solution.py:235
  49.8 25.9 %collective-permute-start.6 = (bf16[64,7168]{1,0:T(8,128)(2,1)S(1)}, bf16[64,7168]{1,0:T(8,128)(2,1)S(1)}, u32[]{:S(2)}, u32[]{:S(2)}) collective-permute-start(bf16[64,7168]{1,0:T(8,128)(2,1)S(1)} %collective-permute-done.5.rest_5_.rest_0_), channel_id=1, source_target_pairs={{0,1},{1,0},{2,3},{3,2},{4,5},{5,4},{6,7},{7,6},{8,9},{9,8},{10,11... | collective-permute-start | bytes 2752520 | tf_op jit(solution)/shard_map/ppermute | solution.py:217
  71.8 3.9 %collective-permute-start.11 = (bf16[64,7168]{1,0:T(8,128)(2,1)S(1)}, bf16[64,7168]{1,0:T(8,128)(2,1)S(1)}, u32[]{:S(2)}, u32[]{:S(2)}) collective-permute-start(bf16[64,7168]{1,0:T(8,128)(2,1)S(1)} %gates.13.rest_2_), channel_id=1, source_target_pairs={{0,1},{1,0},{2,3},{3,2},{4,5},{5,4},{6,7},{7,6},{8,9},{9,8},{10,11... | collective-permute-start | bytes 2752520 | tf_op jit(solution)/shard_map/ppermute | solution.py:217
  71.8 17.0 %collective-permute-start.12 = (bf16[128,1792]{1,0:T(8,128)(2,1)S(1)}, bf16[128,1792]{1,0:T(8,128)(2,1)S(1)}, u32[]{:S(2)}, u32[]{:S(2)}) collective-permute-start(bf16[128,1792]{1,0:T(8,128)(2,1)S(1)} %get-tuple-element.32.refs_1_.rest_5_), channel_id=1, source_target_pairs={{0,16},{8,24},{16,0},{24,8},{1,17},{9,25},{17,1},{25,9},{2,18},{10... | collective-permute-start | bytes 1376264 | tf_op jit(solution)/shard_map/ppermute | solution.py:218
  73.4 15.4 %collective-permute-start.13 = (bf16[128,1792]{1,0:T(8,128)(2,1)S(1)}, bf16[128,1792]{1,0:T(8,128)(2,1)S(1)}, u32[]{:S(2)}, u32[]{:S(2)}) collective-permute-start(bf16[128,1792]{1,0:T(8,128)(2,1)S(1)} %get-tuple-element.34), channel_id=1, source_target_pairs={{0,8},{8,0},{16,24},{24,16},{1,9},{9,1},{17,25},{25,17},{2,10},{10... | collective-permute-start | bytes 1376264 | tf_op jit(solution)/shard_map/ppermute | solution.py:218
  74.9 13.9 %collective-permute-start.14 = (bf16[1024,256]{1,0:T(8,128)(2,1)S(1)}, bf16[1024,256]{1,0:T(8,128)(2,1)S(1)}, u32[]{:S(2)}, u32[]{:S(2)}) collective-permute-start(bf16[1024,256]{1,0:T(8,128)(2,1)S(1)} %get-tuple-element.35), channel_id=1, source_target_pairs={{0,2},{1,3},{2,0},{3,1},{4,6},{5,7},{6,4},{7,5},{8,10},{9,11},{10,... | collective-permute-start | bytes 1572872 | tf_op jit(solution)/shard_map/ppermute | solution.py:242
  89.3 19.2 %collective-permute-start.16 = (bf16[128,1792]{1,0:T(8,128)(2,1)S(1)}, bf16[128,1792]{1,0:T(8,128)(2,1)S(1)}, u32[]{:S(2)}, u32[]{:S(2)}) collective-permute-start(bf16[128,1792]{1,0:T(8,128)(2,1)S(1)} %get-tuple-element.40.rest_5_), channel_id=1, source_target_pairs={{0,8},{8,0},{16,24},{24,16},{1,9},{9,1},{17,25},{25,17},{2,10},{10... | collective-permute-start | bytes 1376264 | tf_op jit(solution)/shard_map/ppermute | solution.py:218
  89.9 21.4 %collective-permute-start.15 = (bf16[128,1792]{1,0:T(8,128)(2,1)S(1)}, bf16[128,1792]{1,0:T(8,128)(2,1)S(1)}, u32[]{:S(2)}, u32[]{:S(2)}) collective-permute-start(bf16[128,1792]{1,0:T(8,128)(2,1)S(1)} %get-tuple-element.43), channel_id=1, source_target_pairs={{0,8},{8,0},{16,24},{24,16},{1,9},{9,1},{17,25},{25,17},{2,10},{10... | collective-permute-start | bytes 1376264 | tf_op jit(solution)/shard_map/ppermute | solution.py:218
  91.4 19.9 %collective-permute-start.17 = (bf16[128,1792]{1,0:T(8,128)(2,1)S(1)}, bf16[128,1792]{1,0:T(8,128)(2,1)S(1)}, u32[]{:S(2)}, u32[]{:S(2)}) collective-permute-start(bf16[128,1792]{1,0:T(8,128)(2,1)S(1)} %get-tuple-element.44.rest_0_), channel_id=1, source_target_pairs={{0,16},{8,24},{16,0},{24,8},{1,17},{9,25},{17,1},{25,9},{2,18},{10... | collective-permute-start | bytes 1376264 | tf_op jit(solution)/shard_map/ppermute | solution.py:218
  91.9 25.5 %collective-permute-start.21 = (bf16[1024,256]{1,0:T(8,128)(2,1)S(1)}, bf16[1024,256]{1,0:T(8,128)(2,1)S(1)}, u32[]{:S(2)}, u32[]{:S(2)}) collective-permute-start(bf16[1024,256]{1,0:T(8,128)(2,1)S(1)} %get-tuple-element.52), channel_id=1, source_target_pairs={{0,4},{1,5},{2,6},{3,7},{4,0},{5,1},{6,2},{7,3},{8,12},{9,13},{10,... | collective-permute-start | bytes 1572872 | tf_op jit(solution)/shard_map/ppermute | solution.py:242
  111.5 11.3 %collective-permute-start.18 = (bf16[128,1792]{1,0:T(8,128)(2,1)S(1)}, bf16[128,1792]{1,0:T(8,128)(2,1)S(1)}, u32[]{:S(2)}, u32[]{:S(2)}) collective-permute-start(bf16[128,1792]{1,0:T(8,128)(2,1)S(1)} %get-tuple-element.47), channel_id=1, source_target_pairs={{0,16},{8,24},{16,0},{24,8},{1,17},{9,25},{17,1},{25,9},{2,18},{10... | collective-permute-start | bytes 1376264 | tf_op jit(solution)/shard_map/ppermute | solution.py:218
  112.2 11.2 %collective-permute-start.19 = (bf16[128,1792]{1,0:T(8,128)(2,1)S(1)}, bf16[128,1792]{1,0:T(8,128)(2,1)S(1)}, u32[]{:S(2)}, u32[]{:S(2)}) collective-permute-start(bf16[128,1792]{1,0:T(8,128)(2,1)S(1)} %get-tuple-element.49), channel_id=1, source_target_pairs={{0,8},{8,0},{16,24},{24,16},{1,9},{9,1},{17,25},{25,17},{2,10},{10... | collective-permute-start | bytes 1376264 | tf_op jit(solution)/shard_map/ppermute | solution.py:218
  117.6 13.5 %collective-permute-start.22 = (bf16[1024,256]{1,0:T(8,128)(2,1)S(1)}, bf16[1024,256]{1,0:T(8,128)(2,1)S(1)}, u32[]{:S(2)}, u32[]{:S(2)}) collective-permute-start(bf16[1024,256]{1,0:T(8,128)(2,1)S(1)} %add_convert_fusion), channel_id=1, source_target_pairs={{0,2},{1,3},{2,0},{3,1},{4,6},{5,7},{6,4},{7,5},{8,10},{9,11},{10,... | collective-permute-start | bytes 1572872 | tf_op jit(solution)/shard_map/ppermute | solution.py:242
  123.5 10.3 %collective-permute-start.20 = (bf16[128,1792]{1,0:T(8,128)(2,1)S(1)}, bf16[128,1792]{1,0:T(8,128)(2,1)S(1)}, u32[]{:S(2)}, u32[]{:S(2)}) collective-permute-start(bf16[128,1792]{1,0:T(8,128)(2,1)S(1)} %get-tuple-element.50), channel_id=1, source_target_pairs={{0,16},{8,24},{16,0},{24,8},{1,17},{9,25},{17,1},{25,9},{2,18},{10... | collective-permute-start | bytes 1376264 | tf_op jit(solution)/shard_map/ppermute | solution.py:218
  124.7 9.8 %collective-permute-start.23 = (bf16[128,1792]{1,0:T(8,128)(2,1)S(1)}, bf16[128,1792]{1,0:T(8,128)(2,1)S(1)}, u32[]{:S(2)}, u32[]{:S(2)}) collective-permute-start(bf16[128,1792]{1,0:T(8,128)(2,1)S(1)} %get-tuple-element.53.rest_2_), channel_id=1, source_target_pairs={{0,8},{8,0},{16,24},{24,16},{1,9},{9,1},{17,25},{25,17},{2,10},{10... | collective-permute-start | bytes 1376264 | tf_op jit(solution)/shard_map/ppermute | solution.py:218
  134.5 12.9 %collective-permute-start.25 = (bf16[128,1792]{1,0:T(8,128)(2,1)S(1)}, bf16[128,1792]{1,0:T(8,128)(2,1)S(1)}, u32[]{:S(2)}, u32[]{:S(2)}) collective-permute-start(bf16[128,1792]{1,0:T(8,128)(2,1)S(1)} %get-tuple-element.55.rest_0_), channel_id=1, source_target_pairs={{0,16},{8,24},{16,0},{24,8},{1,17},{9,25},{17,1},{25,9},{2,18},{10... | collective-permute-start | bytes 1376264 | tf_op jit(solution)/shard_map/ppermute | solution.py:218
  135.8 12.7 %collective-permute-start.26 = (bf16[128,1792]{1,0:T(8,128)(2,1)S(1)}, bf16[128,1792]{1,0:T(8,128)(2,1)S(1)}, u32[]{:S(2)}, u32[]{:S(2)}) collective-permute-start(bf16[128,1792]{1,0:T(8,128)(2,1)S(1)} %get-tuple-element.56.rest_2_), channel_id=1, source_target_pairs={{0,8},{8,0},{16,24},{24,16},{1,9},{9,1},{17,25},{25,17},{2,10},{10... | collective-permute-start | bytes 1376264 | tf_op jit(solution)/shard_map/ppermute | solution.py:218
  (10 other events, 49.8 us)

commit v3 on v2

--- a/solution.py
+++ b/solution.py
@@ -81,10 +81,11 @@
     tokens = rows * len(blocks)
     tile = column_tile(start, width)
     first = start // tile
+    deep = depth // 2
     count = len(blocks)
 
     def kernel(upper_ref, *rest):
-        block_refs, basis_ref = rest[:count], rest[count]
+        block_refs, top_ref, low_ref = rest[:count], rest[count], rest[count + 1]
         keep_ref, send_ref, joint = rest[-3:]
 
         @pl.when(pl.program_id(0) == 0)
@@ -92,7 +93,8 @@
             for i, block_ref in enumerate(block_refs):
                 joint[i * rows : (i + 1) * rows, :] = block_ref[...]
 
-        total = jnp.dot(joint[...], basis_ref[...], preferred_element_type=F32)
+        total = jnp.dot(joint[:, :deep], top_ref[...], preferred_element_type=F32)
+        total += jnp.dot(joint[:, deep:], low_ref[...], preferred_element_type=F32)
         total = total.astype(BF16)
         half = tokens // 2
         is_upper = upper_ref[0] != 0
@@ -106,7 +108,10 @@
             num_scalar_prefetch=1,
             grid=(width // tile,),
             in_specs=[IN_VMEM] * count
-            + [pl.BlockSpec((depth, tile), lambda n, s: (0, first + n))]
+            + [
+                pl.BlockSpec((deep, tile), lambda n, s: (0, first + n)),
+                pl.BlockSpec((deep, tile), lambda n, s: (1, first + n)),
+            ]
             + [ANYWHERE] * len(after),
             out_specs=[pl.BlockSpec((out_rows, tile), lambda n, s: (0, n))] * 2,
             scratch_shapes=[pltpu.VMEM((tokens, depth), BF16)],
@@ -119,7 +124,7 @@
             transcendentals=0,
         ),
         name="chunk_dot",
-    )(jnp.reshape(upper, (1,)), *blocks, basis, *after)
+    )(jnp.reshape(upper, (1,)), *blocks, basis, basis, *after)
 
 
 def first_chunk_dot(blocks, basis, start, width, after, upper):

time: 157 us -> 157 us (level)
  transfers between devices with their start and end apart: 27 -> 27, of which waited for: 14 -> 14; matrix products, arithmetic and copies ran while one was open for 12% -> 12% of each run, Pallas kernels for 30% -> 31%
where the time goes in v3:
time: 157 us; the launch traced here: 156 us
  Pallas kernels  55.5 us (35%)
  waiting for transfers between devices  50.3 us (32%)
  starting transfers between devices  28.5 us (18%)
  matrix products  13.9 us (9%)
  other arithmetic  4.75 us (3%)
  local copies, waits for them, and re-layouts  3.19 us (2%)
    pallas_call x3, Pallas kernels, chunk_dot(): pl.pallas_call(kernel, grid_spec=pltpu.PrefetchScalarGridSpec(num_scalar_...  40 us
    ppermute x15, waiting for transfers between devices, local(): lax.ppermute(x, 'row', [(r, r ^ bit) for r in range(rows_n)])  25.4 us
    ppermute x15, starting transfers between devices, local(): lax.ppermute(x, 'row', [(r, r ^ bit) for r in range(rows_n)])  18.9 us
    ppermute x3, waiting for transfers between devices, local(): block = lax.ppermute(blocks[-1], 'col', ring)  15.8 us
    pallas_call x2, Pallas kernels, lambda_product(): pl.pallas_call(kernel, grid_spec=pltpu.PrefetchScalarGridSpec(num_scalar_...  15.4 us
    dot_general x1, matrix products, first_chunk_dot(): jnp.dot(gate(jnp.concatenate(blocks, axis=0), *after), basis[:, start:sta...  11.5 us
    ppermute x3, waiting for transfers between devices, local(): lax.ppermute(x, 'col', on_both_cores([(c, c ^ bit) for c in range(chips)]))  9 us
    ppermute x3, starting transfers between devices, local(): lax.ppermute(x, 'col', on_both_cores([(c, c ^ bit) for c in range(chips)]))  4.42 us
  transfers between devices with their start and end apart: 27, of which 14 were waited for; matrix products, arithmetic and copies ran while one was open for 12% of the time, Pallas kernels for 31%

profile of v3, /device:TPU:0, one launch (start us, length us, event | category | flops | bytes accessed | tf_op | source)
XLA Modules:
  0.0 156.4 jit_solution(9185742223329411536)
XLA Ops:
  0.5 2.6 %collective-permute-start = (bf16[64,7168]{1,0:T(8,128)(2,1)}, bf16[64,7168]{1,0:T(8,128)(2,1)S(1)}, u32[]{:S(2)}, u32[]{:S(2)}) collective-permute-start(bf16[64,7168]{1,0:T(8,128)(2,1)} %rest_0_.1), channel_id=1, source_target_pairs={{0,2},{1,3},{2,6},{3,7},{4,0},{5,1},{6,4},{7,5},{8,10},{9,11},{10,... | collective-permute-start | bytes 2752520 | tf_op jit(solution)/shard_map/ppermute | solution.py:240
  4.0 2.7 %collective-permute-start.4 = (bf16[128,1024]{1,0:T(8,128)(2,1)S(1)}, bf16[128,1024]{1,0:T(8,128)(2,1)S(1)}, u32[]{:S(2)}, u32[]{:S(2)}) collective-permute-start(bf16[128,1024]{1,0:T(8,128)(2,1)S(1)} %copy_gate.1), channel_id=1, source_target_pairs={{0,8},{8,0},{16,24},{24,16},{1,9},{9,1},{17,25},{25,17},{2,10},{10... | collective-permute-start | bytes 786440 | tf_op jit(solution)/shard_map/ppermute | solution.py:223
  9.0 4.7 %collective-permute-done.4 = bf16[128,1024]{1,0:T(8,128)(2,1)S(1)} collective-permute-done((bf16[128,1024]{1,0:T(8,128)(2,1)S(1)}, bf16[128,1024]{1,0:T(8,128)(2,1)S(1)}, u32[]{:S(2)}, u32[]{:S(2)}) %collective-permute-start.4) | collective-permute-done | bytes 262176 | tf_op jit(solution)/shard_map/ppermute | solution.py:223
  13.9 6.5 %collective-permute-done.3 = bf16[128,1024]{1,0:T(8,128)(2,1)S(1)} collective-permute-done((bf16[128,1024]{1,0:T(8,128)(2,1)S(1)}, bf16[128,1024]{1,0:T(8,128)(2,1)S(1)}, u32[]{:S(2)}, u32[]{:S(2)}) %collective-permute-start.3) | collective-permute-done | bytes 262176 | tf_op jit(solution)/shard_map/ppermute | solution.py:223
  21.0 4.3 %collective-permute-done.refs_0_ = bf16[64,7168]{1,0:T(8,128)(2,1)S(1)} collective-permute-done((bf16[64,7168]{1,0:T(8,128)(2,1)}, bf16[64,7168]{1,0:T(8,128)(2,1)S(1)}, u32[]{:S(2)}, u32[]{:S(2)}) %collective-permute-start) | collective-permute-done | bytes 917536 | tf_op jit(solution)/shard_map/ppermute | solution.py:240
  26.2 2.4 %convolution_bitcast_fusion = f32[2048,512]{1,0:T(8,128)S(1)} fusion(bf16[512,1024]{1,0:T(8,128)(2,1)S(1)} %maximum_select_fusion.refs_1_, bf16[1024,2048]{1,0:T(8,128)(2,1)S(1)} %copy-done.6), kind=kOutput, calls=%fused_computation.3 | convolution fusion | flops 2147483648 | bytes 9437184 | tf_op jit(solution)/shard_map/dot_general | solution.py:265
  30.8 11.5 %fusion.2 = bf16[256,1792]{1,0:T(8,128)(2,1)S(1)} fusion(bf16[256,7168]{1,0:T(8,128)(2,1)S(1)} %gates.11, bf16[7168,3584]{1,0:T(8,128)(2,1)} %rest_5_.5), kind=kOutput, calls=%fused_computation.4 | convolution fusion | flops 6577127424 | bytes 30277632 | tf_op jit(solution)/shard_map/dot_general | solution.py:131
  42.4 1.6 %collective-permute-start.9 = (bf16[128,1792]{1,0:T(8,128)(2,1)S(1)}, bf16[128,1792]{1,0:T(8,128)(2,1)S(1)}, u32[]{:S(2)}, u32[]{:S(2)}) collective-permute-start(bf16[128,1792]{1,0:T(8,128)(2,1)S(1)} %broadcast_select_fusion.rest_7_), channel_id=1, source_target_pairs={{0,16},{8,24},{16,0},{24,8},{1,17},{9,25},{17,1},{25,9},{2,18},{10... | collective-permute-start | bytes 1376264 | tf_op jit(solution)/shard_map/ppermute | solution.py:223
  44.0 4.9 %collective-permute-done.5.rest_6_.rest_0_ = bf16[64,7168]{1,0:T(8,128)(2,1)S(1)} collective-permute-done((bf16[64,7168]{1,0:T(8,128)(2,1)S(1)}, bf16[64,7168]{1,0:T(8,128)(2,1)S(1)}, u32[]{:S(2)}, u32[]{:S(2)}) %collective-permute-start.5) | collective-permute-done | bytes 917536 | tf_op jit(solution)/shard_map/ppermute | solution.py:240
  49.8 13.4 %chunk_dot.3 = (bf16[128,1792]{1,0:T(8,128)(2,1)S(1)}, bf16[128,1792]{1,0:T(8,128)(2,1)S(1)}) custom-call(s32[1]{0:T(128)} %bitcast.2.upper_ref, bf16[64,7168]{1,0:T(8,128)(2,1)S(1)} %copy-done, bf16[64,7168]{1,0:T(8,128)(2,1)S(1)} %collective-permute-done.1.after_ref.rest_1_, bf16[64,7168]{1,0:T(8,128)(2,1)S(1)} %gates.10.rest_2_, ...), custom_call_target="tpu_custom_call" | custom-call | flops 6576668672 | bytes 25690112 | tf_op jit(solution)/shard_map/chunk_dot/pallas_call | solution.py:105
  63.2 1.7 %convert_add_fusion = f32[2048,256]{1,0:T(8,128)S(1)} fusion(bf16[2048,256]{1,0:T(8,128)(2,1)} %collective-permute-done.10, f32[2048,512]{1,0:T(8,128)S(1)} %copy-done.3, pred[]{:T(512)S(6)} %eq.4), kind=kLoop, calls=%fused_computation.5 | loop fusion | flops 1572864 | bytes 7340033 | tf_op jit(solution)/shard_map/add | solution.py:275
  65.2 6.6 %collective-permute-done.7.refs_0_ = bf16[64,7168]{1,0:T(8,128)(2,1)S(1)} collective-permute-done((bf16[64,7168]{1,0:T(8,128)(2,1)S(1)}, bf16[64,7168]{1,0:T(8,128)(2,1)S(1)}, u32[]{:S(2)}, u32[]{:S(2)}) %collective-permute-start.7) | collective-permute-done | bytes 917536 | tf_op jit(solution)/shard_map/ppermute | solution.py:240
  75.7 13.2 %chunk_dot.4 = (bf16[128,1792]{1,0:T(8,128)(2,1)S(1)}, bf16[128,1792]{1,0:T(8,128)(2,1)S(1)}) custom-call(s32[1]{0:T(128)} %bitcast.1.upper_ref, bf16[64,7168]{1,0:T(8,128)(2,1)S(1)} %collective-permute-done.5.rest_6_.rest_0_, bf16[64,7168]{1,0:T(8,128)(2,1)S(1)} %collective-permute-done.6.rest_1_, bf16[64,7168]{1,0:T(8,128)(2,1)S(1)} %gates.13.rest_2_, ...), custom_call_target="tpu_custom_call" | custom-call | flops 6576668672 | bytes 25690112 | tf_op jit(solution)/shard_map/chunk_dot/pallas_call | solution.py:105
  92.0 3.4 %collective-permute-start.21 = (bf16[1024,256]{1,0:T(8,128)(2,1)S(1)}, bf16[1024,256]{1,0:T(8,128)(2,1)S(1)}, u32[]{:S(2)}, u32[]{:S(2)}) collective-permute-start(bf16[1024,256]{1,0:T(8,128)(2,1)S(1)} %get-tuple-element.52), channel_id=1, source_target_pairs={{0,4},{1,5},{2,6},{3,7},{4,0},{5,1},{6,2},{7,3},{8,12},{9,13},{10,... | collective-permute-start | bytes 1572872 | tf_op jit(solution)/shard_map/ppermute | solution.py:247
  95.4 13.4 %chunk_dot.5 = (bf16[128,1792]{1,0:T(8,128)(2,1)S(1)}, bf16[128,1792]{1,0:T(8,128)(2,1)S(1)}) custom-call(s32[1]{0:T(128)} %bitcast.1.upper_ref, bf16[64,7168]{1,0:T(8,128)(2,1)S(1)} %collective-permute-done.5.rest_6_.rest_0_, bf16[64,7168]{1,0:T(8,128)(2,1)S(1)} %collective-permute-done.6.rest_1_, bf16[64,7168]{1,0:T(8,128)(2,1)S(1)} %gates.13.rest_2_, ...), custom_call_target="tpu_custom_call" | custom-call | flops 6576668672 | bytes 25690112 | tf_op jit(solution)/shard_map/chunk_dot/pallas_call | solution.py:105
  108.8 2.6 %collective-permute-done.15.refs_0_ = bf16[128,1792]{1,0:T(8,128)(2,1)S(1)} collective-permute-done((bf16[128,1792]{1,0:T(8,128)(2,1)S(1)}, bf16[128,1792]{1,0:T(8,128)(2,1)S(1)}, u32[]{:S(2)}, u32[]{:S(2)}) %collective-permute-start.15) | collective-permute-done | bytes 458784 | tf_op jit(solution)/shard_map/ppermute | solution.py:223
  113.9 3.7 %collective-permute-done.21 = bf16[1024,256]{1,0:T(8,128)(2,1)S(1)} collective-permute-done((bf16[1024,256]{1,0:T(8,128)(2,1)S(1)}, bf16[1024,256]{1,0:T(8,128)(2,1)S(1)}, u32[]{:S(2)}, u32[]{:S(2)}) %collective-permute-start.21) | collective-permute-done | bytes 524320 | tf_op jit(solution)/shard_map/ppermute | solution.py:247
  118.0 4.9 %collective-permute-done.18 = bf16[128,1792]{1,0:T(8,128)(2,1)S(1)} collective-permute-done((bf16[128,1792]{1,0:T(8,128)(2,1)S(1)}, bf16[128,1792]{1,0:T(8,128)(2,1)S(1)}, u32[]{:S(2)}, u32[]{:S(2)}) %collective-permute-start.18) | collective-permute-done | bytes 458784 | tf_op jit(solution)/shard_map/ppermute | solution.py:223
  125.9 5.3 %collective-permute-done.22 = bf16[1024,256]{1,0:T(8,128)(2,1)S(1)} collective-permute-done((bf16[1024,256]{1,0:T(8,128)(2,1)S(1)}, bf16[1024,256]{1,0:T(8,128)(2,1)S(1)}, u32[]{:S(2)}, u32[]{:S(2)}) %collective-permute-start.22) | collective-permute-done | bytes 524320 | tf_op jit(solution)/shard_map/ppermute | solution.py:247
  131.5 2.5 %collective-permute-done.20 = bf16[128,1792]{1,0:T(8,128)(2,1)S(1)} collective-permute-done((bf16[128,1792]{1,0:T(8,128)(2,1)S(1)}, bf16[128,1792]{1,0:T(8,128)(2,1)S(1)}, u32[]{:S(2)}, u32[]{:S(2)}) %collective-permute-start.20) | collective-permute-done | bytes 458784 | tf_op jit(solution)/shard_map/ppermute | solution.py:223
  136.0 1.7 %collective-permute-start.26 = (bf16[128,1792]{1,0:T(8,128)(2,1)S(1)}, bf16[128,1792]{1,0:T(8,128)(2,1)S(1)}, u32[]{:S(2)}, u32[]{:S(2)}) collective-permute-start(bf16[128,1792]{1,0:T(8,128)(2,1)S(1)} %get-tuple-element.56.rest_2_), channel_id=1, source_target_pairs={{0,8},{8,0},{16,24},{24,16},{1,9},{9,1},{17,25},{25,17},{2,10},{10... | collective-permute-start | bytes 1376264 | tf_op jit(solution)/shard_map/ppermute | solution.py:223
  137.8 7.7 %lambda_product.2.rest_4_ = bf16[2048,3584]{1,0:T(8,128)(2,1)} custom-call(s32[8]{0:T(128)S(1)} %dynamic-slice_bitcast_fusion.refs_2_.place_ref, bf16[2048,256]{1,0:T(8,128)(2,1)S(1)} %get-tuple-element.54.own_ref, bf16[2048,256]{1,0:T(8,128)(2,1)S(1)} %collective-permute-done.24.sib_ref, bf16[128,1792]{1,0:T(8,128)(2,1)S(1)} %get-tuple-element.44.rest_0_, ...), custom_call_target="tpu_custom_call" | custom-call | flops 3758096384 | bytes 7340032 | tf_op jit(solution)/shard_map/lambda_product/pallas_call | solution.py:166
  145.5 2.1 %collective-permute-done.25.rest_1_ = bf16[128,1792]{1,0:T(8,128)(2,1)S(1)} collective-permute-done((bf16[128,1792]{1,0:T(8,128)(2,1)S(1)}, bf16[128,1792]{1,0:T(8,128)(2,1)S(1)}, u32[]{:S(2)}, u32[]{:S(2)}) %collective-permute-start.25) | collective-permute-done | bytes 458784 | tf_op jit(solution)/shard_map/ppermute | solution.py:223
  148.7 7.7 %lambda_product.3 = bf16[2048,3584]{1,0:T(8,128)(2,1)} custom-call(s32[8]{0:T(128)S(1)} %dynamic-slice_bitcast_fusion.refs_2_.place_ref, bf16[2048,256]{1,0:T(8,128)(2,1)S(1)} %get-tuple-element.54.own_ref, bf16[2048,256]{1,0:T(8,128)(2,1)S(1)} %collective-permute-done.24.sib_ref, ...), custom_call_target="tpu_custom_call", output_to_operand_aliasing={{}: (7, {})} | custom-call | flops 3758096384 | bytes 7340032 | tf_op jit(solution)/shard_map/lambda_product/pallas_call | solution.py:166
  (81 shorter events, 25.0 us)
Async XLA Ops:
  0.5 24.8 %collective-permute-start = (bf16[64,7168]{1,0:T(8,128)(2,1)}, bf16[64,7168]{1,0:T(8,128)(2,1)S(1)}, u32[]{:S(2)}, u32[]{:S(2)}) collective-permute-start(bf16[64,7168]{1,0:T(8,128)(2,1)} %rest_0_.1), channel_id=1, source_target_pairs={{0,2},{1,3},{2,6},{3,7},{4,0},{5,1},{6,4},{7,5},{8,10},{9,11},{10,... | collective-permute-start | bytes 2752520 | tf_op jit(solution)/shard_map/ppermute | solution.py:240
  4.0 9.7 %collective-permute-start.4 = (bf16[128,1024]{1,0:T(8,128)(2,1)S(1)}, bf16[128,1024]{1,0:T(8,128)(2,1)S(1)}, u32[]{:S(2)}, u32[]{:S(2)}) collective-permute-start(bf16[128,1024]{1,0:T(8,128)(2,1)S(1)} %copy_gate.1), channel_id=1, source_target_pairs={{0,8},{8,0},{16,24},{24,16},{1,9},{9,1},{17,25},{25,17},{2,10},{10... | collective-permute-start | bytes 786440 | tf_op jit(solution)/shard_map/ppermute | solution.py:223
  6.7 13.7 %collective-permute-start.3 = (bf16[128,1024]{1,0:T(8,128)(2,1)S(1)}, bf16[128,1024]{1,0:T(8,128)(2,1)S(1)}, u32[]{:S(2)}, u32[]{:S(2)}) collective-permute-start(bf16[128,1024]{1,0:T(8,128)(2,1)S(1)} %copy_gate.1), channel_id=1, source_target_pairs={{0,16},{8,24},{16,0},{24,8},{1,17},{9,25},{17,1},{25,9},{2,18},{10... | collective-permute-start | bytes 786440 | tf_op jit(solution)/shard_map/ppermute | solution.py:223
  8.2 12.2 %collective-permute-start.2 = (bf16[128,1024]{1,0:T(8,128)(2,1)S(1)}, bf16[128,1024]{1,0:T(8,128)(2,1)S(1)}, u32[]{:S(2)}, u32[]{:S(2)}) collective-permute-start(bf16[128,1024]{1,0:T(8,128)(2,1)S(1)} %copy_gate.1), channel_id=1, source_target_pairs={{0,24},{8,16},{16,8},{24,0},{1,25},{9,17},{17,9},{25,1},{2,26},{10... | collective-permute-start | bytes 786440 | tf_op jit(solution)/shard_map/ppermute | solution.py:223
  25.3 23.7 %collective-permute-start.5 = (bf16[64,7168]{1,0:T(8,128)(2,1)S(1)}, bf16[64,7168]{1,0:T(8,128)(2,1)S(1)}, u32[]{:S(2)}, u32[]{:S(2)}) collective-permute-start(bf16[64,7168]{1,0:T(8,128)(2,1)S(1)} %gates.10.rest_2_), channel_id=1, source_target_pairs={{0,2},{1,3},{2,6},{3,7},{4,0},{5,1},{6,4},{7,5},{8,10},{9,11},{10,... | collective-permute-start | bytes 2752520 | tf_op jit(solution)/shard_map/ppermute | solution.py:240
  28.8 34.4 %collective-permute-start.10 = (bf16[2048,256]{1,0:T(8,128)(2,1)S(1)}, bf16[2048,256]{1,0:T(8,128)(2,1)}, u32[]{:S(2)}, u32[]{:S(2)}) collective-permute-start(bf16[2048,256]{1,0:T(8,128)(2,1)S(1)} %select_convert_fusion.refs_1_), channel_id=1, source_target_pairs={{0,1},{1,0},{2,3},{3,2},{4,5},{5,4},{6,7},{7,6},{8,9},{9,8},{10,11... | collective-permute-start | bytes 3145736 | tf_op jit(solution)/shard_map/ppermute | solution.py:222
  42.4 22.6 %collective-permute-start.9 = (bf16[128,1792]{1,0:T(8,128)(2,1)S(1)}, bf16[128,1792]{1,0:T(8,128)(2,1)S(1)}, u32[]{:S(2)}, u32[]{:S(2)}) collective-permute-start(bf16[128,1792]{1,0:T(8,128)(2,1)S(1)} %broadcast_select_fusion.rest_7_), channel_id=1, source_target_pairs={{0,16},{8,24},{16,0},{24,8},{1,17},{9,25},{17,1},{25,9},{2,18},{10... | collective-permute-start | bytes 1376264 | tf_op jit(solution)/shard_map/ppermute | solution.py:223
  48.9 22.9 %collective-permute-start.7 = (bf16[64,7168]{1,0:T(8,128)(2,1)S(1)}, bf16[64,7168]{1,0:T(8,128)(2,1)S(1)}, u32[]{:S(2)}, u32[]{:S(2)}) collective-permute-start(bf16[64,7168]{1,0:T(8,128)(2,1)S(1)} %collective-permute-done.5.rest_6_.rest_0_), channel_id=1, source_target_pairs={{0,2},{1,3},{2,6},{3,7},{4,0},{5,1},{6,4},{7,5},{8,10},{9,11},{10,... | collective-permute-start | bytes 2752520 | tf_op jit(solution)/shard_map/ppermute | solution.py:240
  49.8 25.9 %collective-permute-start.6 = (bf16[64,7168]{1,0:T(8,128)(2,1)S(1)}, bf16[64,7168]{1,0:T(8,128)(2,1)S(1)}, u32[]{:S(2)}, u32[]{:S(2)}) collective-permute-start(bf16[64,7168]{1,0:T(8,128)(2,1)S(1)} %collective-permute-done.5.rest_6_.rest_0_), channel_id=1, source_target_pairs={{0,1},{1,0},{2,3},{3,2},{4,5},{5,4},{6,7},{7,6},{8,9},{9,8},{10,11... | collective-permute-start | bytes 2752520 | tf_op jit(solution)/shard_map/ppermute | solution.py:222
  71.8 3.9 %collective-permute-start.11 = (bf16[64,7168]{1,0:T(8,128)(2,1)S(1)}, bf16[64,7168]{1,0:T(8,128)(2,1)S(1)}, u32[]{:S(2)}, u32[]{:S(2)}) collective-permute-start(bf16[64,7168]{1,0:T(8,128)(2,1)S(1)} %gates.13.rest_2_), channel_id=1, source_target_pairs={{0,1},{1,0},{2,3},{3,2},{4,5},{5,4},{6,7},{7,6},{8,9},{9,8},{10,11... | collective-permute-start | bytes 2752520 | tf_op jit(solution)/shard_map/ppermute | solution.py:222
  71.8 17.1 %collective-permute-start.12 = (bf16[128,1792]{1,0:T(8,128)(2,1)S(1)}, bf16[128,1792]{1,0:T(8,128)(2,1)S(1)}, u32[]{:S(2)}, u32[]{:S(2)}) collective-permute-start(bf16[128,1792]{1,0:T(8,128)(2,1)S(1)} %get-tuple-element.32.refs_1_.rest_6_), channel_id=1, source_target_pairs={{0,16},{8,24},{16,0},{24,8},{1,17},{9,25},{17,1},{25,9},{2,18},{10... | collective-permute-start | bytes 1376264 | tf_op jit(solution)/shard_map/ppermute | solution.py:223
  73.4 15.5 %collective-permute-start.13 = (bf16[128,1792]{1,0:T(8,128)(2,1)S(1)}, bf16[128,1792]{1,0:T(8,128)(2,1)S(1)}, u32[]{:S(2)}, u32[]{:S(2)}) collective-permute-start(bf16[128,1792]{1,0:T(8,128)(2,1)S(1)} %get-tuple-element.34), channel_id=1, source_target_pairs={{0,8},{8,0},{16,24},{24,16},{1,9},{9,1},{17,25},{25,17},{2,10},{10... | collective-permute-start | bytes 1376264 | tf_op jit(solution)/shard_map/ppermute | solution.py:223
  74.9 14.0 %collective-permute-start.14 = (bf16[1024,256]{1,0:T(8,128)(2,1)S(1)}, bf16[1024,256]{1,0:T(8,128)(2,1)S(1)}, u32[]{:S(2)}, u32[]{:S(2)}) collective-permute-start(bf16[1024,256]{1,0:T(8,128)(2,1)S(1)} %get-tuple-element.35), channel_id=1, source_target_pairs={{0,2},{1,3},{2,0},{3,1},{4,6},{5,7},{6,4},{7,5},{8,10},{9,11},{10,... | collective-permute-start | bytes 1572872 | tf_op jit(solution)/shard_map/ppermute | solution.py:247
  89.4 19.3 %collective-permute-start.16 = (bf16[128,1792]{1,0:T(8,128)(2,1)S(1)}, bf16[128,1792]{1,0:T(8,128)(2,1)S(1)}, u32[]{:S(2)}, u32[]{:S(2)}) collective-permute-start(bf16[128,1792]{1,0:T(8,128)(2,1)S(1)} %get-tuple-element.40.rest_6_), channel_id=1, source_target_pairs={{0,8},{8,0},{16,24},{24,16},{1,9},{9,1},{17,25},{25,17},{2,10},{10... | collective-permute-start | bytes 1376264 | tf_op jit(solution)/shard_map/ppermute | solution.py:223
  90.0 21.4 %collective-permute-start.15 = (bf16[128,1792]{1,0:T(8,128)(2,1)S(1)}, bf16[128,1792]{1,0:T(8,128)(2,1)S(1)}, u32[]{:S(2)}, u32[]{:S(2)}) collective-permute-start(bf16[128,1792]{1,0:T(8,128)(2,1)S(1)} %get-tuple-element.43), channel_id=1, source_target_pairs={{0,8},{8,0},{16,24},{24,16},{1,9},{9,1},{17,25},{25,17},{2,10},{10... | collective-permute-start | bytes 1376264 | tf_op jit(solution)/shard_map/ppermute | solution.py:223
  91.5 19.9 %collective-permute-start.17 = (bf16[128,1792]{1,0:T(8,128)(2,1)S(1)}, bf16[128,1792]{1,0:T(8,128)(2,1)S(1)}, u32[]{:S(2)}, u32[]{:S(2)}) collective-permute-start(bf16[128,1792]{1,0:T(8,128)(2,1)S(1)} %get-tuple-element.44.rest_0_), channel_id=1, source_target_pairs={{0,16},{8,24},{16,0},{24,8},{1,17},{9,25},{17,1},{25,9},{2,18},{10... | collective-permute-start | bytes 1376264 | tf_op jit(solution)/shard_map/ppermute | solution.py:223
  92.0 25.5 %collective-permute-start.21 = (bf16[1024,256]{1,0:T(8,128)(2,1)S(1)}, bf16[1024,256]{1,0:T(8,128)(2,1)S(1)}, u32[]{:S(2)}, u32[]{:S(2)}) collective-permute-start(bf16[1024,256]{1,0:T(8,128)(2,1)S(1)} %get-tuple-element.52), channel_id=1, source_target_pairs={{0,4},{1,5},{2,6},{3,7},{4,0},{5,1},{6,2},{7,3},{8,12},{9,13},{10,... | collective-permute-start | bytes 1572872 | tf_op jit(solution)/shard_map/ppermute | solution.py:247
  111.7 11.3 %collective-permute-start.18 = (bf16[128,1792]{1,0:T(8,128)(2,1)S(1)}, bf16[128,1792]{1,0:T(8,128)(2,1)S(1)}, u32[]{:S(2)}, u32[]{:S(2)}) collective-permute-start(bf16[128,1792]{1,0:T(8,128)(2,1)S(1)} %get-tuple-element.47), channel_id=1, source_target_pairs={{0,16},{8,24},{16,0},{24,8},{1,17},{9,25},{17,1},{25,9},{2,18},{10... | collective-permute-start | bytes 1376264 | tf_op jit(solution)/shard_map/ppermute | solution.py:223
  112.4 11.2 %collective-permute-start.19 = (bf16[128,1792]{1,0:T(8,128)(2,1)S(1)}, bf16[128,1792]{1,0:T(8,128)(2,1)S(1)}, u32[]{:S(2)}, u32[]{:S(2)}) collective-permute-start(bf16[128,1792]{1,0:T(8,128)(2,1)S(1)} %get-tuple-element.49), channel_id=1, source_target_pairs={{0,8},{8,0},{16,24},{24,16},{1,9},{9,1},{17,25},{25,17},{2,10},{10... | collective-permute-start | bytes 1376264 | tf_op jit(solution)/shard_map/ppermute | solution.py:223
  117.8 13.5 %collective-permute-start.22 = (bf16[1024,256]{1,0:T(8,128)(2,1)S(1)}, bf16[1024,256]{1,0:T(8,128)(2,1)S(1)}, u32[]{:S(2)}, u32[]{:S(2)}) collective-permute-start(bf16[1024,256]{1,0:T(8,128)(2,1)S(1)} %add_convert_fusion), channel_id=1, source_target_pairs={{0,2},{1,3},{2,0},{3,1},{4,6},{5,7},{6,4},{7,5},{8,10},{9,11},{10,... | collective-permute-start | bytes 1572872 | tf_op jit(solution)/shard_map/ppermute | solution.py:247
  123.7 10.3 %collective-permute-start.20 = (bf16[128,1792]{1,0:T(8,128)(2,1)S(1)}, bf16[128,1792]{1,0:T(8,128)(2,1)S(1)}, u32[]{:S(2)}, u32[]{:S(2)}) collective-permute-start(bf16[128,1792]{1,0:T(8,128)(2,1)S(1)} %get-tuple-element.50), channel_id=1, source_target_pairs={{0,16},{8,24},{16,0},{24,8},{1,17},{9,25},{17,1},{25,9},{2,18},{10... | collective-permute-start | bytes 1376264 | tf_op jit(solution)/shard_map/ppermute | solution.py:223
  124.9 9.8 %collective-permute-start.23 = (bf16[128,1792]{1,0:T(8,128)(2,1)S(1)}, bf16[128,1792]{1,0:T(8,128)(2,1)S(1)}, u32[]{:S(2)}, u32[]{:S(2)}) collective-permute-start(bf16[128,1792]{1,0:T(8,128)(2,1)S(1)} %get-tuple-element.53.rest_2_), channel_id=1, source_target_pairs={{0,8},{8,0},{16,24},{24,16},{1,9},{9,1},{17,25},{25,17},{2,10},{10... | collective-permute-start | bytes 1376264 | tf_op jit(solution)/shard_map/ppermute | solution.py:223
  134.7 12.9 %collective-permute-start.25 = (bf16[128,1792]{1,0:T(8,128)(2,1)S(1)}, bf16[128,1792]{1,0:T(8,128)(2,1)S(1)}, u32[]{:S(2)}, u32[]{:S(2)}) collective-permute-start(bf16[128,1792]{1,0:T(8,128)(2,1)S(1)} %get-tuple-element.55.rest_0_), channel_id=1, source_target_pairs={{0,16},{8,24},{16,0},{24,8},{1,17},{9,25},{17,1},{25,9},{2,18},{10... | collective-permute-start | bytes 1376264 | tf_op jit(solution)/shard_map/ppermute | solution.py:223
  136.0 12.7 %collective-permute-start.26 = (bf16[128,1792]{1,0:T(8,128)(2,1)S(1)}, bf16[128,1792]{1,0:T(8,128)(2,1)S(1)}, u32[]{:S(2)}, u32[]{:S(2)}) collective-permute-start(bf16[128,1792]{1,0:T(8,128)(2,1)S(1)} %get-tuple-element.56.rest_2_), channel_id=1, source_target_pairs={{0,8},{8,0},{16,24},{24,16},{1,9},{9,1},{17,25},{25,17},{2,10},{10... | collective-permute-start | bytes 1376264 | tf_op jit(solution)/shard_map/ppermute | solution.py:223
  (10 other events, 54.9 us)
